TPU v7x, 32 devices: a whole 2x2x4 slice. The times are simulated.
32 devices in a mesh: dp: 8 (over y, x, core), inner: 4 (over z).
Axes of the slice: x: 2, y: 2, z: 4, core: 2. Of those that a mesh axis runs over, the one named last changes fastest.
Arguments:
- frames_in: bfloat16 [32, 1024, 1024], P(('dp', 'inner')), may hold values from -6 to 6
- lengths: int32 [32], P(('dp', 'inner')), may hold values from 1 to 1024, 24576 in all
- first_gain: float32 [1024], replicated, may hold values from 0.1 to 1.9
- first_shift: float32 [1024], replicated, may hold values from -3 to 3
- attend_weight: bfloat16 [1024, 3072], P('dp', 'inner'), may hold values from -0.1875 to 0.1875
- attend_bias: float32 [2, 1024], replicated, may hold values from -3 to 3
- output_weight: bfloat16 [1024, 1024], P('dp', 'inner'), may hold values from -3 to 3
- output_bias: float32 [1024], replicated, may hold values from -3 to 3
- second_gain: float32 [1024], replicated, may hold values from 0.1 to 1.9
- second_shift: float32 [1024], replicated, may hold values from -3 to 3
- up_weight: bfloat16 [1024, 4096], P('dp', 'inner'), may hold values from -0.1875 to 0.1875
- up_bias: float32 [4096], replicated, may hold values from -3 to 3
- down_weight: bfloat16 [4096, 1024], P('dp', 'inner'), may hold values from -0.125 to 0.125
- down_bias: float32 [1024], replicated, may hold values from -3 to 3
- cotangent: bfloat16 [32, 1024, 1024], P(('dp', 'inner')), may hold values from -6 to 6
Outputs:
- frames_out: bfloat16 [32, 1024, 1024], P(('dp', 'inner'))
- gradient_frames: bfloat16 [32, 1024, 1024], P(('dp', 'inner'))
- gradient_first_gain: float32 [1024], replicated
- gradient_first_shift: float32 [1024], replicated
- gradient_attend_weight: float32 [1024, 3072], P('dp', 'inner')
- gradient_attend_bias: float32 [2, 1024], replicated
- gradient_output_weight: float32 [1024, 1024], P('dp', 'inner')
- gradient_output_bias: float32 [1024], replicated
- gradient_second_gain: float32 [1024], replicated
- gradient_second_shift: float32 [1024], replicated
- gradient_up_weight: float32 [1024, 4096], P('dp', 'inner')
- gradient_up_bias: float32 [4096], replicated
- gradient_down_weight: float32 [4096, 1024], P('dp', 'inner')
- gradient_down_bias: float32 [1024], replicated
Inputs may be any that keep to these rules, and one draw needn't show every extreme that they name: The longest utterance fills its slot of 1024 frames exactly, and the lengths fill three quarters of all slots.
All inputs are finite; a program needn't handle non-finite values. No bound on the sum of `lengths` on one device may be relied on, other than what follows from the above.
Results may differ from a plain program's by a relative error of at most 0.012.
Values may be sent and summed in bfloat16 or wider, within the bound.
No kernel may reach another device: no remote copies, remote signals or barrier semaphores. Data moves between devices by JAX's collectives and lax.ppermute only.
A program may use at most 320 MiB of HBM per device.

v0:
```python
import jax
import jax.numpy as jnp
from jax import lax
from jax.sharding import PartitionSpec as P

HEADS = 16


def layer_norm(tokens, norm_gain, norm_shift):
    center = tokens - jnp.mean(tokens, axis=-1, keepdims=True)
    spread = jnp.mean(center * center, axis=-1, keepdims=True)
    return center * lax.rsqrt(spread + 1e-05) * norm_gain + norm_shift


def exact_gelu(values):
    return jax.nn.gelu(values, approximate=False)


def contract_rows(left, right):
    return lax.dot_general(
        left, right, (((0,), (0,)), ((), ())), preferred_element_type=jnp.float32
    )


def contract_cols(left, right):
    return lax.dot_general(
        left, right, (((1,), (1,)), ((), ())), preferred_element_type=jnp.float32
    )


def visible_mask(first_row, block_rows, extent, length):
    query_place = first_row + lax.broadcasted_iota(jnp.int32, (block_rows, extent), 0)
    key_place = lax.broadcasted_iota(jnp.int32, (block_rows, extent), 1)
    return (key_place <= query_place) & (key_place < length)


def split_heads(project, frame_count, model_width):
    head_dim = model_width // HEADS
    return tuple(
        (
            project[:, section * model_width : (section + 1) * model_width].reshape(
                frame_count, HEADS, head_dim
            )
            for section in range(3)
        )
    )


def attention_forward(project, lengths, frame_count, model_width):
    block_rows = min(512, frame_count)
    scaling = (model_width // HEADS) ** (-0.5)
    pieces = []
    totals = []
    queries, key_heads, value_heads = split_heads(project, frame_count, model_width)
    for first_row in range(0, frame_count, block_rows):
        extent = first_row + block_rows
        scores = (
            jnp.einsum(
                "qhd,khd->hqk",
                queries[first_row:extent],
                key_heads[:extent],
                preferred_element_type=jnp.float32,
            )
            * scaling
        )
        allowed = visible_mask(first_row, block_rows, extent, lengths[0])
        scores = jnp.where(allowed[None], scores, -1e30)
        highest = jnp.max(scores, axis=-1, keepdims=True)
        weights = jnp.exp(scores - highest)
        summed = jnp.sum(weights, axis=-1, keepdims=True)
        chances = (weights / summed).astype(jnp.bfloat16)
        mixture = jnp.einsum(
            "hqk,khd->qhd", chances, value_heads[:extent], preferred_element_type=jnp.float32
        )
        pieces.append(mixture.reshape(block_rows, model_width))
        totals.append(highest + jnp.log(summed))
    return (jnp.concatenate(pieces, 0), totals)


def attention_backward(project, d_mixture, lengths, totals, frame_count, model_width):
    block_rows = min(512, frame_count)
    head_dim = model_width // HEADS
    scaling = head_dim ** (-0.5)
    counter = 0
    queries, key_heads, value_heads = split_heads(project, frame_count, model_width)
    upstream = d_mixture.reshape(frame_count, HEADS, head_dim)
    d_keys = jnp.zeros(key_heads.shape, jnp.float32)
    d_values = jnp.zeros(value_heads.shape, jnp.float32)
    d_queries = []
    for first_row in range(0, frame_count, block_rows):
        extent = first_row + block_rows
        query_block = queries[first_row:extent]
        up_block = upstream[first_row:extent]
        scores = (
            jnp.einsum(
                "qhd,khd->hqk", query_block, key_heads[:extent], preferred_element_type=jnp.float32
            )
            * scaling
        )
        allowed = visible_mask(first_row, block_rows, extent, lengths[0])
        scores = jnp.where(allowed[None], scores, -1e30)
        chances = jnp.exp(scores - totals[counter])
        counter = counter + 1
        d_chances = jnp.einsum(
            "qhd,khd->hqk", up_block, value_heads[:extent], preferred_element_type=jnp.float32
        )
        center = jnp.sum(chances * d_chances, axis=-1, keepdims=True)
        d_scores = (chances * (d_chances - center)).astype(jnp.bfloat16)
        d_values = d_values.at[:extent].add(
            jnp.einsum(
                "hqk,qhd->khd",
                chances.astype(jnp.bfloat16),
                up_block,
                preferred_element_type=jnp.float32,
            )
        )
        d_queries.append(
            jnp.einsum(
                "hqk,khd->qhd", d_scores, key_heads[:extent], preferred_element_type=jnp.float32
            )
            * scaling
        )
        d_keys = d_keys.at[:extent].add(
            jnp.einsum("hqk,qhd->khd", d_scores, query_block, preferred_element_type=jnp.float32)
            * scaling
        )
    results = jnp.concatenate(
        [
            jnp.concatenate(d_queries, 0).reshape(frame_count, model_width),
            d_keys.reshape(frame_count, model_width),
            d_values.reshape(frame_count, model_width),
        ],
        1,
    )
    return results


def fetch_attention(attend_weight, output_weight):
    column_full = (
        lax.all_gather(attend_weight, "inner", axis=1, tiled=True),
        lax.all_gather(output_weight, "inner", axis=1, tiled=True),
    )
    return (
        lax.all_gather(column_full[0], "dp", axis=0, tiled=True),
        lax.all_gather(column_full[1], "dp", axis=0, tiled=True),
    )


def fetch_feed(up_weight, down_weight):
    column_full = (
        lax.all_gather(up_weight, "inner", axis=1, tiled=True),
        lax.all_gather(down_weight, "inner", axis=1, tiled=True),
    )
    return (
        lax.all_gather(column_full[0], "dp", axis=0, tiled=True),
        lax.all_gather(column_full[1], "dp", axis=0, tiled=True),
    )


def attention_inputs(tokens, lengths, norm_gain, norm_shift, full_attend, attend_bias):
    model_width = tokens.shape[1]
    normed = layer_norm(tokens, norm_gain, norm_shift).astype(jnp.bfloat16)
    bias_row = jnp.concatenate([attend_bias[0], jnp.zeros_like(attend_bias[0]), attend_bias[1]])
    project = (jnp.dot(normed, full_attend, preferred_element_type=jnp.float32) + bias_row).astype(
        jnp.bfloat16
    )
    mixture, totals = attention_forward(
        project, lengths, tokens.shape[0] // lengths.shape[0], model_width
    )
    return (normed, project, mixture.astype(jnp.bfloat16), totals)


def feed_hidden(middle, norm_gain, norm_shift, full_up, up_bias):
    normed_two = layer_norm(middle, norm_gain, norm_shift).astype(jnp.bfloat16)
    hidden = jnp.dot(normed_two, full_up, preferred_element_type=jnp.float32) + up_bias
    active = exact_gelu(hidden).astype(jnp.bfloat16)
    return (normed_two, hidden, active)


def shards(
    frames_in,
    lengths,
    first_gain,
    first_shift,
    attend_weight,
    attend_bias,
    output_weight,
    output_bias,
    second_gain,
    second_shift,
    up_weight,
    up_bias,
    down_weight,
    down_bias,
    cotangent,
):
    utterances, frame_count, model_width = frames_in.shape
    row_total = utterances * frame_count
    tokens = frames_in.reshape(row_total, model_width).astype(jnp.float32)
    full_attend, full_output = fetch_attention(attend_weight, output_weight)
    full_up, full_down = fetch_feed(up_weight, down_weight)
    normed, project, mixture, totals = attention_inputs(
        tokens, lengths, first_gain, first_shift, full_attend, attend_bias
    )
    middle = (
        tokens + jnp.dot(mixture, full_output, preferred_element_type=jnp.float32) + output_bias
    )
    normed_two, hidden, active = feed_hidden(middle, second_gain, second_shift, full_up, up_bias)
    result = jnp.dot(active, full_down, preferred_element_type=jnp.float32) + down_bias
    frames_out = (
        (middle + result).astype(jnp.bfloat16).reshape(utterances, frame_count, model_width)
    )
    column_attend = (
        lax.all_gather(attend_weight, "inner", axis=1, tiled=True),
        lax.all_gather(output_weight, "inner", axis=1, tiled=True),
    )
    back_attend, back_output = (
        lax.all_gather(column_attend[0], "dp", axis=0, tiled=True),
        lax.all_gather(column_attend[1], "dp", axis=0, tiled=True),
    )
    column_feed = (
        lax.all_gather(up_weight, "inner", axis=1, tiled=True),
        lax.all_gather(down_weight, "inner", axis=1, tiled=True),
    )
    back_up, back_down = (
        lax.all_gather(column_feed[0], "dp", axis=0, tiled=True),
        lax.all_gather(column_feed[1], "dp", axis=0, tiled=True),
    )
    live = lax.broadcasted_iota(jnp.int32, (utterances, frame_count), 1) < lengths[:, None]
    masked = jnp.where(live[:, :, None], cotangent, jnp.zeros_like(cotangent))
    d_result = masked.reshape(row_total, model_width)
    upstream = d_result.astype(jnp.float32)
    normed_two, hidden, active = feed_hidden(middle, second_gain, second_shift, back_up, up_bias)
    grad_down_bias = jnp.sum(d_result, axis=0, dtype=jnp.float32)
    grad_down = contract_rows(active, d_result)
    d_active = contract_cols(d_result, back_down)
    gelu_value, gelu_pull = jax.vjp(exact_gelu, hidden)
    d_hidden = gelu_pull(d_active)[0].astype(jnp.bfloat16)
    grad_up_bias = jnp.sum(d_hidden, axis=0, dtype=jnp.float32)
    grad_up = contract_rows(normed_two, d_hidden)
    d_normed_two = contract_cols(d_hidden, back_up)
    norm_value, norm_pull = jax.vjp(layer_norm, middle, second_gain, second_shift)
    d_middle_part, grad_second_gain, grad_second_shift = norm_pull(d_normed_two)
    d_middle = upstream + d_middle_part
    up_wide, down_wide = (
        lax.psum_scatter(grad_up, "dp", scatter_dimension=0, tiled=True),
        lax.psum_scatter(grad_down, "dp", scatter_dimension=0, tiled=True),
    )
    up_owned, down_owned = (
        lax.psum_scatter(up_wide, "inner", scatter_dimension=1, tiled=True),
        lax.psum_scatter(down_wide, "inner", scatter_dimension=1, tiled=True),
    )
    normed, project, mixture, totals = attention_inputs(
        tokens, lengths, first_gain, first_shift, back_attend, attend_bias
    )
    d_branch = d_middle.astype(jnp.bfloat16)
    grad_output_bias = jnp.sum(d_branch, axis=0, dtype=jnp.float32)
    grad_output = contract_rows(mixture, d_branch)
    d_mixture = contract_cols(d_branch, back_output).astype(jnp.bfloat16)
    d_project = attention_backward(
        project, d_mixture, lengths, totals, frame_count, model_width
    ).astype(jnp.bfloat16)
    project_sums = jnp.sum(d_project, axis=0, dtype=jnp.float32)
    grad_attend_bias = jnp.stack([project_sums[:model_width], project_sums[2 * model_width :]], 0)
    grad_attend = contract_rows(normed, d_project)
    d_normed = contract_cols(d_project, back_attend)
    first_value, first_pull = jax.vjp(layer_norm, tokens, first_gain, first_shift)
    d_token_part, grad_first_gain, grad_first_shift = first_pull(d_normed)
    gradient_frames = (
        (d_middle + d_token_part).astype(jnp.bfloat16).reshape(utterances, frame_count, model_width)
    )
    attend_wide, output_wide = (
        lax.psum_scatter(grad_attend, "dp", scatter_dimension=0, tiled=True),
        lax.psum_scatter(grad_output, "dp", scatter_dimension=0, tiled=True),
    )
    attend_owned, output_owned = (
        lax.psum_scatter(attend_wide, "inner", scatter_dimension=1, tiled=True),
        lax.psum_scatter(output_wide, "inner", scatter_dimension=1, tiled=True),
    )
    small = lax.psum(
        (
            grad_first_gain,
            grad_first_shift,
            grad_attend_bias,
            grad_output_bias,
            grad_second_gain,
            grad_second_shift,
            grad_up_bias,
            grad_down_bias,
        ),
        ("dp", "inner"),
    )
    return (
        frames_out,
        gradient_frames,
        small[0],
        small[1],
        attend_owned,
        small[2],
        output_owned,
        small[3],
        small[4],
        small[5],
        up_owned,
        small[6],
        down_owned,
        small[7],
    )


def solution(mesh):
    return jax.shard_map(
        shards,
        mesh=mesh,
        in_specs=(
            P(("dp", "inner"), None, None),
            P(("dp", "inner")),
            P(),
            P(),
            P("dp", "inner"),
            P(),
            P("dp", "inner"),
            P(),
            P(),
            P(),
            P("dp", "inner"),
            P(),
            P("dp", "inner"),
            P(),
            P(("dp", "inner"), None, None),
        ),
        out_specs=(
            P(("dp", "inner"), None, None),
            P(("dp", "inner"), None, None),
            P(),
            P(),
            P("dp", "inner"),
            P(),
            P("dp", "inner"),
            P(),
            P(),
            P(),
            P("dp", "inner"),
            P(),
            P("dp", "inner"),
            P(),
        ),
        check_vma=False,
    )
```

profile of v0, /device:TPU:0, one launch (start us, length us, event | category | flops | bytes accessed | tf_op | source)
XLA Modules:
  0.0 988.6 jit_solution(11154433384407904995)
XLA Ops:
  8.7 27.2 %all_gather.32 = bf16[128,3072]{1,0:T(8,128)(2,1)} all-gather(bf16[128,768]{1,0:T(8,128)(2,1)} %param.31), channel_id=1, replica_groups=mesh['dp'=8,'inner'=4] {'inner'}, dimensions={1}, use_global_device_ids=true | all-gather | bytes 983040 | tf_op jit(solution)/shard_map/all_gather | solution.py:140
  36.0 18.0 %all_gather.34 = bf16[128,1024]{1,0:T(8,128)(2,1)} all-gather(bf16[128,256]{1,0:T(8,128)(2,1)} %param.33), channel_id=1, replica_groups=mesh['dp'=8,'inner'=4] {'inner'}, dimensions={1}, use_global_device_ids=true | all-gather | bytes 327680 | tf_op jit(solution)/shard_map/all_gather | solution.py:141
  58.2 4.7 copy.63
  65.8 15.1 %all-gather.15.cloned.1.call-done = bf16[512,1024]{1,0:T(8,128)(2,1)} async-done(((bf16[512,256]{1,0:T(8,128)(2,1)}), bf16[512,1024]{1,0:T(8,128)(2,1)}) %all-gather.15.cloned.1.call-update) | async-done | bytes 1048592 | tf_op jit(solution)/shard_map/all_gather | solution.py:152
  81.2 45.5 %all-gather.7.cloned.1.call-done = bf16[1024,3072]{1,0:T(8,128)(2,1)} async-done(((bf16[128,3072]{1,0:T(8,128)(2,1)}), bf16[1024,3072]{1,0:T(8,128)(2,1)}) %all-gather.7.cloned.1.call-update) | async-done | bytes 6291472 | tf_op jit(solution)/shard_map/all_gather | solution.py:144
  126.8 10.3 %add_convert_fusion.1 = bf16[1024,3072]{1,0:T(8,128)(2,1)S(1)} fusion(f32[3072]{0:T(1024)S(1)} %pad_maximum_fusion.5, bf16[1024,3072]{1,0:T(8,128)(2,1)} %all-gather.7.cloned.1.call-done, bf16[1,1024,1024]{1,2,0:T(8,128)(2,1)S(1)} %copy.54, f32[1024]{0:T(1024)S(1)} %copy-done.57, f32[1024]{0:T(1024)S(1)} %copy-done.40, f32[1024]{0:T(1024)S(1)} %fusion.58, ...), kind=kOutput, calls=%fused_computation.38 | convolution fusion | flops 6455033856 | bytes 14708736 | tf_op jit(solution)/shard_map/dot_general | solution.py:164
  141.4 3.9 copy.61
  153.2 3.9 copy.59
  157.2 10.8 %fusion.79 = (f32[16,512]{1,0:T(8,128)S(1)}, f32[16,512,512]{1,2,0:T(8,128)}) fusion(bf16[512,16,64]{0,2,1:T(8,128)(2,1)} %bitcast.150, bf16[512,16,64]{0,2,1:T(8,128)(2,1)} %bitcast.139, pred[512,512]{0,1:T(8,128)(4,1)S(1)} %fusion.56), kind=kOutput, calls=%fused_computation.133 | convolution fusion | flops 549445632 | bytes 19169280 | tf_op jit(solution)/shard_map/qhd,khd->hqk/dot_general | solution.py:58
  168.0 8.3 fusion.12
  176.3 16.8 %fusion.78 = (f32[16,512]{1,0:T(8,128)S(1)}, f32[16,512,1024]{2,1,0:T(8,128)}) fusion(bf16[512,16,64]{0,2,1:T(8,128)(2,1)S(1)} %bitcast.137, bf16[1024,16,64]{0,2,1:T(8,128)(2,1)} %bitcast.135, pred[512,1024]{1,0:T(8,128)(4,1)S(1)} %copy-done.20), kind=kOutput, calls=%fused_computation.132 | convolution fusion | flops 1098899456 | bytes 37257216 | tf_op jit(solution)/shard_map/qhd,khd->hqk/dot_general | solution.py:58
  193.2 15.4 %fusion = f32[16,512]{1,0:T(8,128)S(1)} fusion(f32[16,512,1024]{2,1,0:T(8,128)} %get-tuple-element.139, f32[16,512]{1,0:T(8,128)S(1)} %get-tuple-element.138), kind=kLoop, calls=%fused_computation.6 | loop fusion | flops 16769024 | bytes 33619968 | tf_op jit(solution)/shard_map/reduce_sum | solution.py:70
  208.6 14.0 %fusion.50 = bf16[16,64,512]{2,1,0:T(8,128)(2,1)S(1)} fusion(bf16[1024,16,64]{0,2,1:T(8,128)(2,1)S(1)} %bitcast.141, f32[16,512,1024]{2,1,0:T(8,128)} %get-tuple-element.139, f32[16,512]{1,0:T(8,128)S(1)} %fusion, f32[16,512]{1,0:T(8,128)S(1)} %get-tuple-element.138), kind=kOutput, calls=%fused_computation.92 | convolution fusion | flops 1099431936 | bytes 36765696 | tf_op jit(solution)/shard_map/hqk,khd->qhd/dot_general | solution.py:72
  224.4 4.0 fusion.49
  228.4 4.5 fusion.80
  237.0 49.2 %multiply_convert_fusion.2 = (bf16[1024,4096]{1,0:T(8,128)(2,1)}, f32[1024,4096]{1,0:T(8,128)}, f32[1024,4096]{1,0:T(8,128)}) fusion(f32[4096]{0:T(1024)S(1)} %copy-done.55, bf16[1024,4096]{1,0:T(8,128)(2,1)} %all-gather.13.cloned.1.call-done, bf16[1024,1024]{0,1:T(8,128)(2,1)} %add_convert_fusion.6.clone.4), kind=kOutput, calls=%fused_computation.17 | convolution fusion | flops 8866758656 | bytes 52445184 | tf_op jit(solution)/shard_map/dot_general | solution.py:175
  286.2 24.1 %convert_reduce_fusion = (f32[4096]{0:T(1024)}, bf16[1024,4096]{1,0:T(8,128)(2,1)}) fusion(f32[1024,4096]{1,0:T(8,128)} %get-tuple-element.123, bf16[4096,1024]{1,0:T(8,128)(2,1)} %all-gather.17.cloned.1.call-done, bf16[1,1024,1024]{1,2,0:T(8,128)(2,1)S(1)} %copy-done.11, pred[1024]{0:T(1024)(128)(4,1)S(1)} %copy-done.48, ...), kind=kOutput, calls=%fused_computation.11 | convolution fusion | flops 8662282240 | bytes 52462592 | tf_op jit(solution)/shard_map/dot_general | solution.py:26
  310.4 15.9 %fusion.82 = (f32[1024]{0:T(1024)}, f32[1024,1024]{1,0:T(8,128)}) fusion(bf16[1024,4096]{1,0:T(8,128)(2,1)} %get-tuple-element.154, bf16[1024,4096]{1,0:T(8,128)(2,1)} %all-gather.13.cloned.1.call-done), kind=kOutput, calls=%fused_computation.136 | convolution fusion | flops 8590982144 | bytes 20975616 | tf_op jit(solution)/shard_map/dot_general | solution.py:26
  326.2 5.4 copy.64
  331.7 5.4 multiply_reduce_fusion.2
  343.5 4.4 fusion.53
  348.0 3.9 convolution_convert_fusion
  353.9 23.3 %multiply_reduce_fusion = (f32[16,512]{1,0:T(8,128)S(1)}, f32[16,512,1024]{2,1,0:T(8,128)}) fusion(f32[16,512,1024]{2,1,0:T(8,128)} %get-tuple-element.139, f32[16,512]{1,0:T(8,128)S(1)} %copy-done.24, bf16[512,16,64]{0,2,1:T(8,128)(2,1)S(1)} %bitcast.143, bf16[1024,16,64]{0,2,1:T(8,128)(2,1)S(1)} %bitcast.142), kind=kOutput, calls=%fused_computation.1 | convolution fusion | flops 1098899456 | bytes 70320128 | tf_op jit(solution)/shard_map/qhd,khd->hqk/dot_general | solution.py:104
  377.2 28.4 %multiply_convert_fusion = bf16[16,512,1024]{2,1,0:T(8,128)(2,1)} fusion(f32[16,512,1024]{2,1,0:T(8,128)} %get-tuple-element.148, f32[16,512,1024]{2,1,0:T(8,128)} %get-tuple-element.139, f32[16,512]{1,0:T(8,128)S(1)} %get-tuple-element.147, f32[16,512]{1,0:T(8,128)S(1)} %copy-done.24), kind=kLoop, calls=%fused_computation | loop fusion | flops 33554432 | bytes 83951616 | tf_op jit(solution)/shard_map/convert_element_type | solution.py:108
  405.5 12.0 %fusion.52 = bf16[512,16,64]{0,2,1:T(8,128)(2,1)} fusion(bf16[1024,16,64]{0,2,1:T(8,128)(2,1)S(1)} %bitcast.136, bf16[16,512,1024]{2,1,0:T(8,128)(2,1)} %multiply_convert_fusion), kind=kOutput, calls=%fused_computation.94 | convolution fusion | flops 1074790400 | bytes 19922944 | tf_op jit(solution)/shard_map/hqk,khd->qhd/dot_general | solution.py:118
  417.6 14.4 %multiply_reduce_fusion.1 = (f32[16,512]{1,0:T(8,128)}, f32[16,512,512]{1,2,0:T(8,128)}) fusion(f32[16,512,512]{1,2,0:T(8,128)} %get-tuple-element.141, f32[16,512]{1,0:T(8,128)} %log_add_fusion.1, bf16[512,16,64]{0,2,1:T(8,128)(2,1)S(1)} %bitcast.149, bf16[512,16,64]{0,2,1:T(8,128)(2,1)} %bitcast.158), kind=kOutput, calls=%fused_computation.14 | convolution fusion | flops 549445632 | bytes 35717120 | tf_op jit(solution)/shard_map/qhd,khd->hqk/dot_general | solution.py:104
  434.3 8.0 multiply_convert_fusion.1
  445.6 4.0 multiply_bitcast_fusion
  449.5 5.5 fusion.46
  455.0 11.0 %fusion.33 = bf16[1024,16,64]{0,2,1:T(8,128)(2,1)} fusion(f32[512,16,64]{0,2,1:T(8,128)} %multiply_bitcast_fusion, bf16[512,16,64]{0,2,1:T(8,128)(2,1)S(1)} %bitcast.138, bf16[16,512,1024]{2,1,0:T(8,128)(2,1)} %multiply_convert_fusion), kind=kOutput, calls=%fused_computation.66 | convolution fusion | flops 1076887552 | bytes 22020096 | tf_op jit(solution)/shard_map/hqk,qhd->khd/dot_general | solution.py:124
  466.1 15.3 %fusion.32 = bf16[1024,16,64]{0,2,1:T(8,128)(2,1)} fusion(f32[512,16,64]{0,2,1:T(8,128)} %fusion.46, bf16[512,16,64]{0,2,1:T(8,128)(2,1)S(1)} %bitcast.144, f32[16,512,1024]{2,1,0:T(8,128)} %get-tuple-element.139, f32[16,512]{1,0:T(8,128)S(1)} %copy-done.25), kind=kOutput, calls=%fused_computation.64 | convolution fusion | flops 1092616192 | bytes 38830080 | tf_op jit(solution)/shard_map/hqk,qhd->khd/dot_general | solution.py:110
  481.4 14.2 %fusion.64 = f32[1024,3072]{1,0:T(8,128)} fusion(bf16[1,1024,1024]{1,2,0:T(8,128)(2,1)S(1)} %copy-done.1, f32[1024]{0:T(1024)S(1)} %copy-done.58, f32[1024]{0:T(1024)S(1)} %copy-done.41, f32[1024]{0:T(1024)S(1)} %copy-done.37, f32[1024]{0:T(1024)S(1)} %copy-done.27, bf16[1024,1024]{0,1:T(8,128)(2,1)} %bitcast.152, bf16[1024,1024]{0,1:T(8,128)(2,1)} %bitcast.145, ...), kind=kOutput, calls=%fused_computation.122 | convolution fusion | flops 6467616768 | bytes 20987904 | tf_op jit(solution)/shard_map/dot_general | solution.py:20
  496.3 18.5 %fusion.68 = f32[1024,4096]{1,0:T(8,128)} fusion(bf16[1024,4096]{1,0:T(8,128)(2,1)} %get-tuple-element.154, f32[1024,1024]{0,1:T(8,128)} %copy-done.3, f32[1024]{0:T(1024)S(1)} %copy-done.52, f32[1024]{0:T(1024)S(1)} %copy-done.35, f32[1024]{0:T(1024)S(1)} %copy-done.31, f32[1024]{0:T(1024)S(1)} %copy-done.29), kind=kOutput, calls=%fused_computation.124 | convolution fusion | flops 8595177472 | bytes 29376512 | tf_op jit(solution)/shard_map/dot_general | solution.py:20
  515.5 16.4 %fusion.39 = f32[4096,1024]{1,0:T(8,128)} fusion(bf16[1024,4096]{1,0:T(8,128)(2,1)} %get-tuple-element.122, bf16[1,1024,1024]{1,2,0:T(8,128)(2,1)} %copy.63, pred[1024]{0:T(1024)(128)(4,1)S(1)} %copy-done.49), kind=kOutput, calls=%fused_computation.79 | convolution fusion | flops 8590983168 | bytes 27264000 | tf_op jit(solution)/shard_map/dot_general | solution.py:20
  532.7 55.8 %reduce-scatter.9.cloned.1.call-done = f32[128,3072]{1,0:T(8,128)} async-done(((f32[1024,3072]{1,0:T(8,128)}), f32[128,3072]{1,0:T(8,128)}) %reduce-scatter.9.cloned.1.call-update) | async-done | bytes 1572880 | tf_op jit(solution)/shard_map/reduce_scatter | solution.py:273
  588.6 119.9 %reduce-scatter.17.cloned.1.call-done = f32[128,4096]{1,0:T(8,128)} async-done(((f32[1024,4096]{1,0:T(8,128)}), f32[128,4096]{1,0:T(8,128)}) %reduce-scatter.17.cloned.1.call-update) | async-done | bytes 2097168 | tf_op jit(solution)/shard_map/reduce_scatter | solution.py:246
  708.6 15.6 %fusion.37 = bf16[1,1024,1024]{1,2,0:T(8,128)(2,1)} fusion(f32[1024,1024]{0,1:T(8,128)} %copy-done.3, f32[1024]{0:T(1024)S(1)} %copy-done.59, bf16[1024,4096]{1,0:T(8,128)(2,1)} %get-tuple-element.122, bf16[4096,1024]{1,0:T(8,128)(2,1)} %all-gather.17.cloned.1.call-done), kind=kOutput, calls=%fused_computation.75 | convolution fusion | flops 8593080320 | bytes 23072768 | tf_op jit(solution)/shard_map/dot_general | solution.py:209
  724.1 4.2 copy.71
  728.3 100.0 %reduce-scatter.21.cloned.1.call-done = f32[512,1024]{1,0:T(8,128)} async-done(((f32[4096,1024]{1,0:T(8,128)}), f32[512,1024]{1,0:T(8,128)}) %reduce-scatter.21.cloned.1.call-update) | async-done | bytes 2097168 | tf_op jit(solution)/shard_map/reduce_scatter | solution.py:247
  828.3 12.1 %fusion.81 = (f32[1024]{0:T(1024)S(1)}, f32[1024,1024]{1,0:T(8,128)}) fusion(bf16[1024,3072]{1,0:T(8,128)(2,1)} %all-gather.7.cloned.1.call-done, bf16[1024,1024]{0,1:T(8,128)(2,1)} %bitcast.153, bf16[1024,1024]{0,1:T(8,128)(2,1)} %bitcast.146, bf16[1024,1024]{0,1:T(8,128)(2,1)} %bitcast.156), kind=kOutput, calls=%fused_computation.135 | convolution fusion | flops 6462372864 | bytes 16781312 | tf_op jit(solution)/shard_map/dot_general | solution.py:26
  840.4 5.4 copy.68
  845.8 3.1 fusion.30
  851.4 3.6 convert_reduce_fusion.2
  855.1 4.0 copy.72
  859.0 4.6 convert_reduce_fusion.1
  863.7 42.3 %all-reduce.2 = (f32[1024]{0:T(1024)}, f32[1024]{0:T(1024)}, f32[2,1024]{1,0:T(2,128)}, f32[1024]{0:T(1024)}, f32[1024]{0:T(1024)}, /*index=5*/f32[1024]{0:T(1024)}, f32[4096]{0:T(1024)}, f32[1024]{0:T(1024)}) all-reduce(f32[1024]{0:T(1024)S(1)} %get-tuple-element.108, ...), channel_id=1, replica_groups=mesh['dp'=8,'inner'=4] {'dp','inner'}, use_global_device_ids=true, to_apply=%region_15.16 | all-reduce | flops 12288 | bytes 98304 | tf_op jit(solution)/shard_map/psum | solution.py:280
  906.0 29.9 %reduce-scatter.19.cloned.1.call-done = f32[128,1024]{1,0:T(8,128)} async-done(((f32[128,4096]{1,0:T(8,128)}), f32[128,1024]{1,0:T(8,128)}) %reduce-scatter.19.cloned.1.call-update) | async-done | bytes 524304 | tf_op jit(solution)/shard_map/reduce_scatter | solution.py:250
  935.9 45.9 %reduce-scatter.23.cloned.1.call-done = f32[512,256]{1,0:T(8,128)} async-done(((f32[512,1024]{1,0:T(8,128)}), f32[512,256]{1,0:T(8,128)}) %reduce-scatter.23.cloned.1.call-update) | async-done | bytes 524304 | tf_op jit(solution)/shard_map/reduce_scatter | solution.py:251
  (216 shorter events, 44.8 us)
Async XLA Ops:
  7.2 55.7 %copy-start.50 = (f32[2,1024]{1,0:T(2,128)S(1)}, f32[2,1024]{1,0:T(2,128)}, u32[]{:S(2)}) copy-start(f32[2,1024]{1,0:T(2,128)} %param.32) | copy-start | bytes 24580
  7.2 46.8 %all-gather.11.cloned.1.call-start = ((), (), s32[]{:S(2)}) async-start(), calls=%async_computation.10 | async-start | bytes 1310720 | tf_op jit(solution)/shard_map/all_gather | solution.py:151
  7.9 73.1 %all-gather.15.cloned.1.call-start = ((), (), s32[]{:S(2)}) async-start(), calls=%async_computation.12 | async-start | bytes 1310720 | tf_op jit(solution)/shard_map/all_gather | solution.py:152
  8.7 118.1 %all-gather.7.cloned.1.call-start = ((), (), s32[]{:S(2)}) async-start(), calls=%async_computation.8 | async-start | bytes 7077888 | tf_op jit(solution)/shard_map/all_gather | solution.py:144
  35.9 192.5 %all-gather.9.cloned.1.call-start = ((), (), s32[]{:S(2)}) async-start(), calls=%async_computation.9 | async-start | bytes 2359296 | tf_op jit(solution)/shard_map/all_gather | solution.py:145
  54.0 183.0 %all-gather.13.cloned.1.call-start = ((), (), s32[]{:S(2)}) async-start(), calls=%async_computation.11 | async-start | bytes 9437184 | tf_op jit(solution)/shard_map/all_gather | solution.py:155
  54.5 231.7 %all-gather.17.cloned.1.call-start = ((), (), s32[]{:S(2)}) async-start(), calls=%async_computation.13 | async-start | bytes 9437184 | tf_op jit(solution)/shard_map/all_gather | solution.py:156
  55.2 71.5 %copy-start.40 = (f32[1024]{0:T(1024)S(1)}, f32[1024]{0:T(1024)}, u32[]{:S(2)}) copy-start(f32[1024]{0:T(1024)} %param.29) | copy-start | bytes 12292
  55.3 71.5 %copy-start.57 = (f32[1024]{0:T(1024)S(1)}, f32[1024]{0:T(1024)}, u32[]{:S(2)}) copy-start(f32[1024]{0:T(1024)} %param.30) | copy-start | bytes 12292
  58.2 170.3 %copy-start = (bf16[1,1024,1024]{1,2,0:T(8,128)(2,1)}, bf16[1,1024,1024]{1,2,0:T(8,128)(2,1)S(1)}, u32[]{:S(2)}) copy-start(bf16[1,1024,1024]{1,2,0:T(8,128)(2,1)S(1)} %copy.54) | copy-start | bytes 6291460
  62.8 63.9 %copy-start.47 = (pred[1024]{0:T(1024)(128)(4,1)}, pred[1024]{0:T(1024)(128)(4,1)S(1)}, u32[]{:S(2)}) copy-start(pred[1024]{0:T(1024)(128)(4,1)S(1)} %iota_compare_fusion.2) | copy-start | bytes 3076
  63.3 63.5 %copy-start.26 = (f32[1024]{0:T(1024)}, f32[1024]{0:T(1024)S(1)}, u32[]{:S(2)}) copy-start(f32[1024]{0:T(1024)S(1)} %broadcast_multiply_fusion.1) | copy-start | bytes 12292
  64.5 62.3 %copy-start.36 = (f32[1024]{0:T(1024)}, f32[1024]{0:T(1024)S(1)}, u32[]{:S(2)}) copy-start(f32[1024]{0:T(1024)S(1)} %fusion.58) | copy-start | bytes 12292
  81.0 451.0 %reduce-scatter.13.cloned.1.call-start = ((), (), s32[]{:S(2)}) async-start(), calls=%async_computation.16 | async-start | bytes 4718592 | tf_op jit(solution)/shard_map/reduce_scatter | solution.py:274
  148.2 28.1 %copy-start.9 = (bf16[512,1024]{0,1:T(8,128)(2,1)}, bf16[512,1024]{0,1:T(8,128)(2,1)S(1)}, u32[]{:S(2)}) copy-start(bf16[512,1024]{0,1:T(8,128)(2,1)S(1)} %copy.60) | copy-start | bytes 3145732
  193.2 15.4 %copy-start.14 = (bf16[1024,1024]{0,1:T(8,128)(2,1)S(1)}, bf16[1024,1024]{0,1:T(8,128)(2,1)}, u32[]{:S(2)}) copy-start(bf16[1024,1024]{0,1:T(8,128)(2,1)} %copy.59) | copy-start | bytes 6291460
  193.2 29.4 %slice-start = ((s8[16777216]{0:T(1024)(128)(4,1)}), s8[4194304]{0:T(1024)(128)(4,1)S(1)}, s32[]{:S(2)}) async-start(s8[16777216]{0:T(1024)(128)(4,1)} %bitcast.131), calls=%async_computation.22 | async-start | bytes 8388608
  208.5 14.1 %slice-start.1 = ((s8[16777216]{0:T(1024)(128)(4,1)}), s8[4194304]{0:T(1024)(128)(4,1)S(1)}, s32[]{:S(2)}) async-start(s8[16777216]{0:T(1024)(128)(4,1)} %bitcast.131), calls=%async_computation.23 | async-start | bytes 8388608
  208.5 14.1 %slice-start.2 = ((s8[16777216]{0:T(1024)(128)(4,1)}), s8[4194304]{0:T(1024)(128)(4,1)S(1)}, s32[]{:S(2)}) async-start(s8[16777216]{0:T(1024)(128)(4,1)} %bitcast.131), calls=%async_computation.24 | async-start | bytes 8388608
  208.6 15.2 %slice-start.3 = ((s8[16777216]{0:T(1024)(128)(4,1)}), s8[4194304]{0:T(1024)(128)(4,1)S(1)}, s32[]{:S(2)}) async-start(s8[16777216]{0:T(1024)(128)(4,1)} %bitcast.131), calls=%async_computation.25 | async-start | bytes 8388608
  208.6 15.8 %copy-start.21 = (bf16[512,1024]{0,1:T(8,128)(2,1)S(1)}, bf16[512,1024]{0,1:T(8,128)(2,1)}, u32[]{:S(2)}) copy-start(bf16[512,1024]{0,1:T(8,128)(2,1)} %copy.55) | copy-start | bytes 3145732
  233.0 53.2 %copy-start.28 = (f32[1024]{0:T(1024)}, f32[1024]{0:T(1024)S(1)}, u32[]{:S(2)}) copy-start(f32[1024]{0:T(1024)S(1)} %broadcast_multiply_fusion) | copy-start | bytes 12292
  233.5 52.7 %copy-start.42 = (f32[1024]{0:T(1024)}, f32[1024]{0:T(1024)S(1)}, u32[]{:S(2)}) copy-start(f32[1024]{0:T(1024)S(1)} %multiply_reduce_fusion.4) | copy-start | bytes 12292
  233.5 52.7 %copy-start.30 = (f32[1024]{0:T(1024)}, f32[1024]{0:T(1024)S(1)}, u32[]{:S(2)}) copy-start(f32[1024]{0:T(1024)S(1)} %fusion.59) | copy-start | bytes 12292
  237.0 49.2 %copy-start.11 = (bf16[1,1024,1024]{1,2,0:T(8,128)(2,1)S(1)}, bf16[1,1024,1024]{1,2,0:T(8,128)(2,1)}, u32[]{:S(2)}) copy-start(bf16[1,1024,1024]{1,2,0:T(8,128)(2,1)} %copy.63) | copy-start | bytes 6291460
  237.0 49.2 %copy-start.48 = (pred[1024]{0:T(1024)(128)(4,1)S(1)}, pred[1024]{0:T(1024)(128)(4,1)}, u32[]{:S(2)}) copy-start(pred[1024]{0:T(1024)(128)(4,1)} %copy-done.47) | copy-start | bytes 3076
  353.1 24.1 %copy-start.16 = (bf16[512,1024]{0,1:T(8,128)(2,1)}, bf16[512,1024]{0,1:T(8,128)(2,1)S(1)}, u32[]{:S(2)}) copy-start(bf16[512,1024]{0,1:T(8,128)(2,1)S(1)} %get-tuple-element.132) | copy-start | bytes 3145732
  353.1 235.4 %reduce-scatter.9.cloned.1.call-start = ((), (), s32[]{:S(2)}) async-start(), calls=%async_computation.14 | async-start | bytes 14155776 | tf_op jit(solution)/shard_map/reduce_scatter | solution.py:273
  377.2 28.4 %copy-start.8 = (bf16[1024,1024]{0,1:T(8,128)(2,1)S(1)}, bf16[1024,1024]{0,1:T(8,128)(2,1)}, u32[]{:S(2)}) copy-start(bf16[1024,1024]{0,1:T(8,128)(2,1)} %copy.61) | copy-start | bytes 6291460
  405.5 12.0 %copy-start.18 = (bf16[512,1024]{0,1:T(8,128)(2,1)S(1)}, bf16[512,1024]{0,1:T(8,128)(2,1)}, u32[]{:S(2)}) copy-start(bf16[512,1024]{0,1:T(8,128)(2,1)} %get-tuple-element.133) | copy-start | bytes 3145732
  417.6 14.4 %slice-start.4 = ((s8[16777216]{0:T(1024)(128)(4,1)}), s8[4194304]{0:T(1024)(128)(4,1)S(1)}, s32[]{:S(2)}) async-start(s8[16777216]{0:T(1024)(128)(4,1)} %bitcast.133), calls=%async_computation.26 | async-start | bytes 8388608
  417.6 14.4 %slice-start.5 = ((s8[16777216]{0:T(1024)(128)(4,1)}), s8[4194304]{0:T(1024)(128)(4,1)S(1)}, s32[]{:S(2)}) async-start(s8[16777216]{0:T(1024)(128)(4,1)} %bitcast.133), calls=%async_computation.27 | async-start | bytes 8388608
  417.6 15.6 %slice-start.6 = ((s8[16777216]{0:T(1024)(128)(4,1)}), s8[4194304]{0:T(1024)(128)(4,1)S(1)}, s32[]{:S(2)}) async-start(s8[16777216]{0:T(1024)(128)(4,1)} %bitcast.133), calls=%async_computation.28 | async-start | bytes 8388608
  417.6 16.8 %slice-start.7 = ((s8[16777216]{0:T(1024)(128)(4,1)}), s8[4194304]{0:T(1024)(128)(4,1)S(1)}, s32[]{:S(2)}) async-start(s8[16777216]{0:T(1024)(128)(4,1)} %bitcast.133), calls=%async_computation.29 | async-start | bytes 8388608
  455.0 11.0 %copy-start.17 = (bf16[512,1024]{0,1:T(8,128)(2,1)S(1)}, bf16[512,1024]{0,1:T(8,128)(2,1)}, u32[]{:S(2)}) copy-start(bf16[512,1024]{0,1:T(8,128)(2,1)} %copy-done.16) | copy-start | bytes 3145732
  455.0 11.0 %copy-start.25 = (f32[16,512]{1,0:T(8,128)S(1)}, f32[16,512]{1,0:T(8,128)}, u32[]{:S(2)}) copy-start(f32[16,512]{1,0:T(8,128)} %log_add_fusion) | copy-start | bytes 98308
  466.0 15.4 %copy-start.1 = (bf16[1,1024,1024]{1,2,0:T(8,128)(2,1)S(1)}, bf16[1,1024,1024]{1,2,0:T(8,128)(2,1)}, u32[]{:S(2)}) copy-start(bf16[1,1024,1024]{1,2,0:T(8,128)(2,1)} %copy-done) | copy-start | bytes 6291460
  466.0 15.4 %copy-start.27 = (f32[1024]{0:T(1024)S(1)}, f32[1024]{0:T(1024)}, u32[]{:S(2)}) copy-start(f32[1024]{0:T(1024)} %copy-done.26) | copy-start | bytes 12292
  466.0 15.4 %copy-start.37 = (f32[1024]{0:T(1024)S(1)}, f32[1024]{0:T(1024)}, u32[]{:S(2)}) copy-start(f32[1024]{0:T(1024)} %copy-done.36) | copy-start | bytes 12292
  466.0 15.4 %copy-start.41 = (f32[1024]{0:T(1024)S(1)}, f32[1024]{0:T(1024)}, u32[]{:S(2)}) copy-start(f32[1024]{0:T(1024)} %param.29) | copy-start | bytes 12292
  466.1 15.4 %copy-start.58 = (f32[1024]{0:T(1024)S(1)}, f32[1024]{0:T(1024)}, u32[]{:S(2)}) copy-start(f32[1024]{0:T(1024)} %param.30) | copy-start | bytes 12292
  495.7 212.8 %reduce-scatter.17.cloned.1.call-start = ((), (), s32[]{:S(2)}) async-start(), calls=%async_computation.18 | async-start | bytes 18874368 | tf_op jit(solution)/shard_map/reduce_scatter | solution.py:246
  514.8 313.5 %reduce-scatter.21.cloned.1.call-start = ((), (), s32[]{:S(2)}) async-start(), calls=%async_computation.20 | async-start | bytes 18874368 | tf_op jit(solution)/shard_map/reduce_scatter | solution.py:247
  531.9 176.7 %copy-start.59 = (f32[1024]{0:T(1024)S(1)}, f32[1024]{0:T(1024)}, u32[]{:S(2)}) copy-start(f32[1024]{0:T(1024)} %param.40) | copy-start | bytes 12292
  531.9 374.1 %reduce-scatter.15.cloned.1.call-start = ((), (), s32[]{:S(2)}) async-start(), calls=%async_computation.17 | async-start | bytes 655360 | tf_op jit(solution)/shard_map/reduce_scatter | solution.py:278
  532.7 373.4 %reduce-scatter.11.cloned.1.call-start = ((), (), s32[]{:S(2)}) async-start(), calls=%async_computation.15 | async-start | bytes 1966080 | tf_op jit(solution)/shard_map/reduce_scatter | solution.py:277
  588.6 347.4 %reduce-scatter.19.cloned.1.call-start = ((), (), s32[]{:S(2)}) async-start(), calls=%async_computation.19 | async-start | bytes 2621440 | tf_op jit(solution)/shard_map/reduce_scatter | solution.py:250
  708.5 273.4 %reduce-scatter.23.cloned.1.call-start = ((), (), s32[]{:S(2)}) async-start(), calls=%async_computation.21 | async-start | bytes 2621440 | tf_op jit(solution)/shard_map/reduce_scatter | solution.py:251
  (37 other events, 185.1 us)
Sparse Core Ops, SparseCore 0:
  9.6 39.6 all-gather.10
  50.9 30.0 all-gather.14
  82.9 43.8 all-gather.6
  128.5 27.8 all-gather.8
  158.2 54.3 all-gather.12
  214.3 54.3 all-gather.16
  353.2 51.5 reduce-scatter.12
  495.8 92.6 reduce-scatter.8
  592.5 115.9 reduce-scatter.16
  712.3 115.9 reduce-scatter.20
  831.3 21.6 reduce-scatter.14
  855.8 33.9 reduce-scatter.10
  892.8 43.1 reduce-scatter.18
  938.7 43.1 reduce-scatter.22
where the time goes:
time: 993 us; the launch traced here: 989 us
  waiting for transfers between devices  415 us (42%)
  matrix products  322 us (32%)
  other arithmetic  89.4 us (9%)
  blocking collectives  87.4 us (9%)
  local copies, waits for them, and re-layouts  58.9 us (6%)
  between operations  15.6 us (2%)
    reduce_scatter x1, waiting for transfers between devices, shards(): lax.psum_scatter(grad_up, 'dp', scatter_dimension=0, tiled=True)  120 us
    reduce_scatter x1, waiting for transfers between devices, shards(): lax.psum_scatter(grad_down, 'dp', scatter_dimension=0, tiled=True)  100 us
    dot_general x4, matrix products, contract_cols(): lax.dot_general(left, right, (((1,), (1,)), ((), ())), preferred_element_...  56 us
    reduce_scatter x1, waiting for transfers between devices, shards(): lax.psum_scatter(grad_attend, 'dp', scatter_dimension=0, tiled=True)  55.8 us
    dot_general x4, matrix products, contract_rows(): lax.dot_general(left, right, (((0,), (0,)), ((), ())), preferred_element_...  53.5 us
    dot_general x1, matrix products, feed_hidden(): jnp.dot(normed_two, full_up, preferred_element_type=jnp.float32) + up_bias  49.2 us
    reduce_scatter x1, waiting for transfers between devices, shards(): lax.psum_scatter(down_wide, 'inner', scatter_dimension=1, tiled=True)  45.9 us
    all_gather x1, waiting for transfers between devices, fetch_attention(): lax.all_gather(column_full[0], 'dp', axis=0, tiled=True)  45.5 us
  transfers between devices with their start and end apart: 14, of which 7 were waited for; matrix products, arithmetic and copies ran while one was open for 40% of the time, Pallas kernels for 0%

commit v1 on v0

v1 whole, which is shorter than its diff:
```python
import functools

import jax
import jax.numpy as jnp
from jax import lax
from jax.experimental import pallas as pl
from jax.experimental.pallas import tpu as pltpu
from jax.sharding import PartitionSpec as P

HEADS = 16
HEAD = 64
TILE = 1024
ROWS = 256
LOG2E = 1.4426950408889634
MASKED = -1e30
SCALE = HEAD ** (-0.5)
BF = jnp.bfloat16
F32 = jnp.float32
LIMIT = 60 * 2**20


def dot(left, right, on_left, on_right):
    return lax.dot_general(
        left, right, (((on_left,), (on_right,)), ((), ())), preferred_element_type=F32
    )


def normalise(values):
    center = values - jnp.mean(values, axis=-1, keepdims=True)
    spread = jnp.mean(center * center, axis=-1, keepdims=True)
    scale = lax.rsqrt(spread + 1e-05)
    return center * scale, scale


def params(name_limit=LIMIT):
    return pltpu.CompilerParams(vmem_limit_bytes=name_limit)


def estimate(flops, moved, exps=0):
    return pl.CostEstimate(flops=int(flops), bytes_accessed=int(moved), transcendentals=int(exps))


ANY = pl.BlockSpec(memory_space=pl.ANY)
SMEM = pl.BlockSpec(memory_space=pltpu.SMEM)


def whole(*shape):
    return pl.BlockSpec(shape, lambda *_: (0,) * len(shape))


def vec(size):
    return jax.ShapeDtypeStruct((1, size), F32)


PIECES = 8
SLOTS = 4
T_ROW = 0
T_COL = 8
T_SLOT_IN = 12
T_SLOT_OUT = 16
T_PAIR = 20
T_OUT = 24
T_PLACE = 32
T_CORE = 40
T_SIZE = 48


def make_table(spread):
    if not spread:
        order = list(range(4))
        entries = [0] * T_SIZE
        entries[T_PAIR : T_PAIR + 4] = order
        return jnp.array(entries, jnp.int32)
    row = lax.axis_index("dp").astype(jnp.int32)
    column = lax.axis_index("inner").astype(jnp.int32)
    core = row & 1
    near = jnp.where(core == 0, 2, 4)
    far = 6 - near
    entries = [
        row,
        row ^ near,
        row ^ far,
        row ^ 6,
        row ^ 1,
        row ^ 1 ^ far,
        row ^ 1 ^ near,
        row ^ 7,
    ]
    entries += [(column - slot) & 3 for slot in range(4)]
    entries += [(column - block) & 3 for block in range(4)]
    entries += [(block - column) & 3 for block in range(4)]
    pair = row >> 1
    entries += [pair, pair ^ (near >> 1), pair ^ (far >> 1), pair ^ 3]
    for half in range(2):
        a, b = (far, near) if half == 0 else (near, far)
        own = row ^ half
        entries += [own ^ 6, own ^ a, own ^ b, own]
    for half in range(2):
        first = far if half == 0 else near
        for block in range(4):
            relative = (pair ^ block) << 1
            entries.append(
                jnp.where(
                    relative == 6,
                    0,
                    jnp.where(relative == 0, 3, jnp.where(relative == first, 1, 2)),
                )
            )
    entries += [core]
    entries += [jnp.int32(0)] * (T_SIZE - len(entries))
    return jnp.stack([jnp.asarray(entry, jnp.int32) for entry in entries])


def aligned(index, size):
    return pl.ds(pl.multiple_of(index * size, size), size)


def load_columns(pieces, tab, block, target, sems, width, first=0):
    if len(pieces) == 1:
        copies = [
            pltpu.make_async_copy(pieces[0].at[:, aligned(block, width)], target, sems.at[0])
        ]
        return copies
    slot = tab[T_SLOT_IN + block]
    rows = pieces[0].shape[1]
    return [
        pltpu.make_async_copy(
            pieces[p].at[slot, :, pl.ds(first, width)],
            target.at[aligned(tab[T_ROW + p], rows), :],
            sems.at[p],
        )
        for p in range(PIECES)
    ]


def load_rows(pieces, tab, step, target, sems):
    if len(pieces) == 1:
        return [
            pltpu.make_async_copy(
                pieces[0].at[aligned(tab[T_PAIR + step], TILE), :], target, sems.at[0]
            )
        ]
    rows, width = pieces[0].shape[1:]
    partner = (4, 6, 5, 7)[step]
    copies = []
    for n, p in enumerate((step, partner)):
        half = tab[T_ROW + p] & 1
        for slot in range(SLOTS):
            copies.append(
                pltpu.make_async_copy(
                    pieces[p].at[slot],
                    target.at[aligned(half, rows), aligned(tab[T_COL + slot], width)],
                    sems.at[n * SLOTS + slot],
                )
            )
    return copies


def load_all(pieces, tab, target, sems, width, first=0):
    if len(pieces) == 1:
        return [pltpu.make_async_copy(pieces[0], target, sems.at[0])]
    rows = pieces[0].shape[1]
    return [
        pltpu.make_async_copy(
            pieces[p].at[slot, :, pl.ds(first, width)],
            target.at[aligned(tab[T_ROW + p], rows), aligned(tab[T_COL + slot], width)],
            sems.at[p * SLOTS + slot],
        )
        for p in range(PIECES)
        for slot in range(SLOTS)
    ]


def store_column_block(outs, tab, block, source, sems, width, first=0):
    if len(outs) == 1:
        return [pltpu.make_async_copy(source, outs[0].at[:, aligned(block, width)], sems.at[0])]
    rows = outs[0].shape[2]
    slot = tab[T_SLOT_OUT + block]
    return [
        pltpu.make_async_copy(
            source.at[aligned(tab[T_OUT + half * 4 + place], rows), :],
            outs[half].at[place, slot, :, pl.ds(first, width)],
            sems.at[half * 4 + place],
        )
        for half in range(2)
        for place in range(4)
    ]


def store_row_pair(outs, tab, pair, source, sems):
    if len(outs) == 1:
        return [pltpu.make_async_copy(source, outs[0].at[aligned(pair, TILE), :], sems.at[0])]
    rows, width = outs[0].shape[2:]
    copies = []
    for half in range(2):
        local = tab[T_CORE] ^ half
        for block in range(4):
            copies.append(
                pltpu.make_async_copy(
                    source.at[aligned(local, rows), pl.ds(block * width, width)],
                    outs[half].at[tab[T_PLACE + half * 4 + pair], tab[T_SLOT_OUT + block]],
                    sems.at[half * 4 + block],
                )
            )
    return copies


def start(copies):
    for copy in copies:
        copy.start()


def wait(copies):
    for copy in copies:
        copy.wait()


def gradient_shapes(spread, rows, columns, dp, inner):
    if spread:
        return [jax.ShapeDtypeStruct((4, 4, rows // dp, columns // inner), BF)] * 2
    return [jax.ShapeDtypeStruct((rows, columns), BF)]


def project_kernel(count, tab, frames, gain, shift, bias, *rest):
    pieces = rest[:count]
    normed, project, tokens, weight, sems, token_sem = rest[count:]
    step = pl.program_id(0)
    steps = pl.num_programs(0)
    width = project.shape[0]

    def fetch(block):
        slot = lax.rem(block, 2)
        return load_columns(pieces, tab, block, weight.at[slot], sems.at[slot], width)

    @pl.when(step == 0)
    def _():
        copy = pltpu.make_async_copy(frames, tokens, token_sem)
        copy.start()
        start(fetch(step))
        copy.wait()
        for first in range(0, tokens.shape[0], ROWS):
            rows = pl.ds(first, ROWS)
            unit, _ = normalise(tokens[rows, :].astype(F32))
            normed[rows, :] = (unit * gain[...] + shift[...]).astype(BF)

    @pl.when(step + 1 < steps)
    def _():
        start(fetch(step + 1))

    wait(fetch(step))
    column = jnp.transpose(jnp.broadcast_to(bias[...], (128, width)))[:, :1]
    project[...] = (dot(weight[lax.rem(step, 2)], normed[...], 0, 1) + column).astype(BF)


def project_call(tab, frames, gain, shift, bias, pieces):
    frames_count, model = frames.shape
    width = 3 * model // 4
    return pl.pallas_call(
        functools.partial(project_kernel, len(pieces)),
        grid=(4,),
        in_specs=[SMEM, ANY, whole(1, model), whole(1, model)]
        + [pl.BlockSpec((1, width), lambda i: (0, i))]
        + [ANY] * len(pieces),
        out_specs=[whole(frames_count, model), pl.BlockSpec((width, frames_count), lambda i: (i, 0))],
        out_shape=[
            jax.ShapeDtypeStruct((frames_count, model), BF),
            jax.ShapeDtypeStruct((3 * model, frames_count), BF),
        ],
        scratch_shapes=[
            pltpu.VMEM((frames_count, model), BF),
            pltpu.VMEM((2, model, width), BF),
            pltpu.SemaphoreType.DMA((2, 8)),
            pltpu.SemaphoreType.DMA,
        ],
        compiler_params=params(),
        cost_estimate=estimate(6 * frames_count * model * model, 16e6),
        name="project",
    )(tab, frames, gain, shift, bias, *pieces)


def causal_bias(block):
    key = lax.broadcasted_iota(jnp.int32, (block, block), 0)
    query = lax.broadcasted_iota(jnp.int32, (block, block), 1)
    return jnp.where(key <= query, 0.0, MASKED)


def extend_rows(length, extent):
    first = lax.broadcasted_iota(jnp.int32, (16, extent), 0) == 0
    past = lax.broadcasted_iota(jnp.int32, (16, extent), 1) >= length
    key_rows = jnp.where(first & past, MASKED, 0.0).astype(BF)
    query_rows = jnp.where(first, 1.0, 0.0).astype(BF)
    return key_rows, query_rows


def attention_kernel(
    group, block, lengths, query, key, value, mixture, totals, keys, queries, causal
):
    extent = query.shape[1]

    @pl.when(pl.program_id(0) == 0)
    def _():
        causal[...] = causal_bias(block)

    key_rows, query_rows = extend_rows(lengths[0], extent)
    for head in range(group):
        part = pl.ds(HEAD * head, HEAD)
        keys[head, :HEAD, :] = key[part, :]
        keys[head, HEAD:, :] = key_rows
        queries[head, :HEAD, :] = query[part, :]
        queries[head, HEAD:, :] = query_rows
    for head in range(group):
        part = pl.ds(HEAD * head, HEAD)
        for tile in range(extent // block):
            place = pl.ds(tile * block, block)
            own = queries[head, :, place]
            scores = []
            for other in range(tile + 1):
                score = dot(keys[head, :, pl.ds(other * block, block)], own, 0, 0)
                scores.append(score + causal[...] if other == tile else score)
            highest = scores[0].max(0, keepdims=True)
            for score in scores[1:]:
                highest = jnp.maximum(highest, score.max(0, keepdims=True))
            offset = highest * (SCALE * LOG2E)
            summed = jnp.zeros((1, block), F32)
            total = jnp.zeros((HEAD, block), F32)
            for other, score in enumerate(scores):
                weight = jnp.exp2(score * (SCALE * LOG2E) - offset)
                summed = summed + weight.sum(0, keepdims=True)
                total = total + dot(value[part, pl.ds(other * block, block)], weight.astype(BF), 1, 0)
            mixture[part, place] = (total * (1.0 / summed)).astype(BF)
            totals[0, pl.ds(head, 1), place] = offset + jnp.log2(summed)


def attention_call(lengths, project):
    extent = project.shape[1]
    group, block = 2, min(512, extent)
    size, steps = HEAD * group, HEADS // group

    def part(section):
        return pl.BlockSpec((size, extent), lambda i: (i + section * steps, 0))

    pairs = extent * extent * 5 // 8
    return pl.pallas_call(
        functools.partial(attention_kernel, group, block),
        grid=(steps,),
        in_specs=[SMEM, part(0), part(1), part(2)],
        out_specs=[part(0), pl.BlockSpec((1, group, extent), lambda i: (i, 0, 0))],
        out_shape=[
            jax.ShapeDtypeStruct((HEADS * HEAD, extent), BF),
            jax.ShapeDtypeStruct((steps, group, extent), F32),
        ],
        scratch_shapes=[
            pltpu.VMEM((group, HEAD + 16, extent), BF),
            pltpu.VMEM((group, HEAD + 16, extent), BF),
            pltpu.VMEM((block, block), F32),
        ],
        compiler_params=params(),
        cost_estimate=estimate(16 * HEADS * pairs * HEAD, 8e6, HEADS * pairs),
        name="attention",
    )(lengths, project, project, project)


def gelu_parts(hidden):
    chance = 0.5 + 0.5 * lax.erf(hidden * 0.7071067811865476)
    density = jnp.exp2(hidden * hidden * (-0.5 * LOG2E)) * 0.3989422804014327
    return hidden * chance, chance + hidden * density


def up_kernel(counts, tab, lengths, mixture, frames, cotangent, *rest):
    count_out, count_up, count_grad = counts
    out_bias, gain, shift, up_bias = rest[:4]
    out_pieces = rest[4 : 4 + count_out]
    rest = rest[4 + count_out :]
    up_pieces = rest[:count_up]
    rest = rest[count_up:]
    middle, normed, active, slope, down_bias = rest[:5]
    grads = rest[5 : 5 + count_grad]
    (
        mixed,
        out_weight,
        tokens,
        result,
        weight,
        staged,
        sems_in,
        sems_out,
        sems_up,
        sems_grad,
    ) = rest[5 + count_grad :]
    step = pl.program_id(0)
    steps = pl.num_programs(0)
    extent = tokens.shape[0]

    def fetch(block):
        slot = lax.rem(block, 2)
        return load_columns(up_pieces, tab, block, weight.at[slot], sems_up.at[slot], TILE)

    def send(pair):
        slot = lax.rem(pair, 2)
        return store_row_pair(grads, tab, pair, staged.at[slot], sems_grad.at[slot])

    @pl.when(step == 0)
    def _():
        width = mixed.shape[0] // 4
        copies = [pltpu.make_async_copy(mixture, mixed, sems_in.at[0])]
        copies += [pltpu.make_async_copy(frames, tokens, sems_in.at[1])]
        outs = load_all(out_pieces, tab, out_weight, sems_out, width, TILE)
        last = pltpu.make_async_copy(cotangent, result, sems_in.at[2])
        start(copies + outs)
        start(fetch(step))
        last.start()
        wait(copies + outs)
        for first in range(0, extent, ROWS):
            rows = pl.ds(first, ROWS)
            branch = dot(mixed[:, rows], out_weight[...], 0, 0) + out_bias[...]
            total = tokens[rows, :].astype(F32) + branch
            middle[rows, :] = total
            unit, _ = normalise(total)
            normed[rows, :] = (unit * gain[...] + shift[...]).astype(BF)
        last.wait()
        place = lax.broadcasted_iota(jnp.int32, (extent, 1), 0)
        masked = jnp.where(place < lengths[0], result[...].astype(F32), 0.0)
        result[...] = masked.astype(BF)
        down_bias[...] = masked.sum(0, keepdims=True)

    @pl.when(step + 1 < steps)
    def _():
        start(fetch(step + 1))

    wait(fetch(step))
    now = lax.rem(step, 2)
    for first in range(0, extent, ROWS):
        rows = pl.ds(first, ROWS)
        hidden = dot(normed[rows, :], weight[now], 1, 0) + up_bias[...]
        value, grade = gelu_parts(hidden)
        active[rows, :] = value.astype(BF)
        slope[rows, :] = grade.astype(BF)

    @pl.when(step >= 2)
    def _():
        wait(send(step - 2))

    staged[now] = dot(active[...], result[...], 0, 0).astype(BF)
    start(send(step))

    @pl.when(step == steps - 1)
    def _():
        wait(send(step - 1))
        wait(send(step))


def up_call(tab, lengths, mixture, frames, cotangent, vectors, out_pieces, up_pieces, spread, sizes):
    model, extent = mixture.shape
    hidden = 4 * model
    grads = gradient_shapes(spread, hidden, model, *sizes)
    steps = hidden // TILE
    return pl.pallas_call(
        functools.partial(up_kernel, (len(out_pieces), len(up_pieces), len(grads))),
        grid=(steps,),
        in_specs=[SMEM, SMEM, ANY, ANY, ANY]
        + [whole(1, model)] * 3
        + [pl.BlockSpec((1, TILE), lambda i: (0, i))]
        + [ANY] * (len(out_pieces) + len(up_pieces)),
        out_specs=[
            whole(extent, model),
            whole(extent, model),
            pl.BlockSpec((extent, TILE), lambda i: (0, i)),
            pl.BlockSpec((extent, TILE), lambda i: (0, i)),
            whole(1, model),
        ]
        + [ANY] * len(grads),
        out_shape=[
            jax.ShapeDtypeStruct((extent, model), F32),
            jax.ShapeDtypeStruct((extent, model), BF),
            jax.ShapeDtypeStruct((extent, hidden), BF),
            jax.ShapeDtypeStruct((extent, hidden), BF),
            vec(model),
        ]
        + grads,
        scratch_shapes=[
            pltpu.VMEM((model, extent), BF),
            pltpu.VMEM((model, model), BF),
            pltpu.VMEM((extent, model), BF),
            pltpu.VMEM((extent, model), BF),
            pltpu.VMEM((2, model, TILE), BF),
            pltpu.VMEM((2, TILE, model), BF),
            pltpu.SemaphoreType.DMA((3,)),
            pltpu.SemaphoreType.DMA((32,)),
            pltpu.SemaphoreType.DMA((2, 8)),
            pltpu.SemaphoreType.DMA((2, 8)),
        ],
        compiler_params=params(),
        cost_estimate=estimate(18 * extent * model * model, 50e6, extent * hidden),
        name="up",
    )(tab, lengths, mixture, frames, cotangent, *vectors, *out_pieces, *up_pieces)


def back_kernel(counts, tab, lengths, mixture, middle, normed, cotangent, slope, *rest):
    count_out, count_up, count_down, count_grad = counts
    gain = rest[0]
    rest = rest[1:]
    out_pieces, rest = rest[:count_out], rest[count_out:]
    up_pieces, rest = rest[:count_up], rest[count_up:]
    down_pieces, rest = rest[:count_down], rest[count_down:]
    d_middle, d_mixture, up_bias, gain_grad, shift_grad, out_bias = rest[:6]
    rest = rest[6:]
    grads, rest = rest[:count_grad], rest[count_grad:]
    (
        mixed,
        out_weight,
        total,
        unit_rows,
        result,
        down,
        up,
        d_hidden,
        d_normed,
        staged,
        sems_in,
        sems_out,
        sems_down,
        sems_up,
        sems_grad,
    ) = rest
    spread = len(grads[0].shape) == 4
    if spread:
        up_grads = out_grads = grads
    else:
        up_grads, out_grads = grads[:1], grads[1:]
    step = pl.program_id(0)
    steps = pl.num_programs(0)
    extent, model = result.shape
    width = model // 4

    def fetch(index):
        slot = index % 2
        copies = load_rows(down_pieces, tab, index, down.at[slot], sems_down.at[slot])
        block = tab[T_PAIR + index]
        copies += load_columns(up_pieces, tab, block, up.at[slot], sems_up.at[slot], TILE)
        return copies

    def send(index):
        slot = index % 2
        block = tab[T_PAIR + index]
        return store_column_block(
            up_grads, tab, block, staged.at[slot], sems_grad.at[slot], TILE
        )

    def send_out(block):
        return store_column_block(
            out_grads,
            tab,
            block,
            staged.at[0, :, pl.ds(block * width, width)],
            sems_out.at[pl.ds(block * 8, 8)],
            width,
            TILE if spread else 0,
        )

    def early(n):
        pair = ((cotangent, result), (normed, unit_rows))[n]
        return pltpu.make_async_copy(*pair, sems_in.at[n])

    def late():
        return [
            pltpu.make_async_copy(middle, total, sems_in.at[2]),
            pltpu.make_async_copy(mixture, mixed, sems_in.at[3]),
        ] + load_all(out_pieces, tab, out_weight, sems_out, width, TILE)

    def body(index):
        slot = index % 2
        if index == 0:
            early(0).start()
            start(fetch(0))
            early(1).start()
            early(0).wait()
            place = lax.broadcasted_iota(jnp.int32, (extent, 1), 0)
            masked = jnp.where(place < lengths[0], result[...].astype(F32), 0.0)
            result[...] = masked.astype(BF)
        if index == 2:
            start(late())
        if index + 1 < 4:
            start(fetch(index + 1))
        wait(fetch(index))
        sums = jnp.zeros((1, TILE), F32)
        for first in range(0, extent, ROWS):
            rows = pl.ds(first, ROWS)
            d_active = dot(result[rows, :], down[slot], 1, 1)
            piece = (d_active * slope[rows, :].astype(F32)).astype(BF)
            d_hidden[rows, :] = piece
            sums = sums + piece.astype(F32).sum(0, keepdims=True)
        up_bias[...] = sums
        if index == 0:
            early(1).wait()
        if index >= 2:
            wait(send(index - 2))
        staged[slot] = dot(unit_rows[...], d_hidden[...], 0, 0).astype(BF)
        start(send(index))
        part = dot(d_hidden[...], up[slot], 1, 1)
        if index == 0:
            d_normed[...] = part
        else:
            d_normed[...] += part

    for index in range(4):
        pl.when(step == index)(functools.partial(body, index))

    @pl.when(step == steps - 1)
    def _():
        wait(late())
        gains = jnp.zeros((1, model), F32)
        shifts = jnp.zeros((1, model), F32)
        biases = jnp.zeros((1, model), F32)
        for first in range(0, extent, ROWS):
            rows = pl.ds(first, ROWS)
            unit, scale = normalise(total[rows, :])
            grade = d_normed[rows, :]
            gains = gains + (grade * unit).sum(0, keepdims=True)
            shifts = shifts + grade.sum(0, keepdims=True)
            grade = grade * gain[...]
            level = jnp.mean(grade, axis=-1, keepdims=True)
            tilt = jnp.mean(grade * unit, axis=-1, keepdims=True)
            d_total = result[rows, :].astype(F32) + scale * (grade - level - unit * tilt)
            d_middle[rows, :] = d_total
            branch = d_total.astype(BF)
            unit_rows[rows, :] = branch
            biases = biases + branch.astype(F32).sum(0, keepdims=True)
        gain_grad[...] = gains
        shift_grad[...] = shifts
        out_bias[...] = biases
        wait(send(2))
        staged[0] = dot(mixed[...], unit_rows[...], 1, 0).astype(BF)
        for block in range(4):
            start(send_out(block))
        d_mixture[...] = dot(out_weight[...], unit_rows[...], 1, 1).astype(BF)
        wait(send(3))
        for block in range(4):
            wait(send_out(block))


def back_call(
    tab, lengths, mixture, middle, normed, cotangent, slope, gain, pieces, spread, sizes
):
    out_pieces, up_pieces, down_pieces = pieces
    model, extent = mixture.shape
    hidden = slope.shape[1]
    if spread:
        grads = gradient_shapes(spread, model, hidden + model, *sizes)
    else:
        grads = gradient_shapes(spread, model, hidden, *sizes)
        grads += gradient_shapes(spread, model, model, *sizes)
    steps = hidden // TILE
    grid = pltpu.PrefetchScalarGridSpec(
        num_scalar_prefetch=1,
        grid=(steps,),
        in_specs=[SMEM, ANY, ANY, ANY, ANY]
        + [pl.BlockSpec((extent, TILE), lambda i, tab: (0, tab[T_PAIR + i]))]
        + [whole(1, model)]
        + [ANY] * (len(out_pieces) + len(up_pieces) + len(down_pieces)),
        out_specs=[
            whole(extent, model),
            whole(model, extent),
            pl.BlockSpec((1, TILE), lambda i, tab: (0, tab[T_PAIR + i])),
            whole(1, model),
            whole(1, model),
            whole(1, model),
        ]
        + [ANY] * len(grads),
        scratch_shapes=[
            pltpu.VMEM((model, extent), BF),
            pltpu.VMEM((model, model), BF),
            pltpu.VMEM((extent, model), F32),
            pltpu.VMEM((extent, model), BF),
            pltpu.VMEM((extent, model), BF),
            pltpu.VMEM((2, TILE, model), BF),
            pltpu.VMEM((2, model, TILE), BF),
            pltpu.VMEM((extent, TILE), BF),
            pltpu.VMEM((extent, model), F32),
            pltpu.VMEM((2, model, TILE), BF),
            pltpu.SemaphoreType.DMA((4,)),
            pltpu.SemaphoreType.DMA((32,)),
            pltpu.SemaphoreType.DMA((2, 8)),
            pltpu.SemaphoreType.DMA((2, 8)),
            pltpu.SemaphoreType.DMA((2, 8)),
        ],
    )
    return pl.pallas_call(
        functools.partial(
            back_kernel, (len(out_pieces), len(up_pieces), len(down_pieces), len(grads))
        ),
        grid_spec=grid,
        out_shape=[
            jax.ShapeDtypeStruct((extent, model), F32),
            jax.ShapeDtypeStruct((model, extent), BF),
            vec(hidden),
            vec(model),
            vec(model),
            vec(model),
        ]
        + grads,
        compiler_params=params(),
        cost_estimate=estimate(28 * extent * model * model, 60e6),
        name="back",
    )(
        tab,
        lengths,
        mixture,
        middle,
        normed,
        cotangent,
        slope,
        gain,
        *out_pieces,
        *up_pieces,
        *down_pieces,
    )


def attention_back_kernel(
    group,
    block,
    lengths,
    query,
    key,
    value,
    mixture,
    d_mixture,
    totals,
    d_project,
    keys,
    queries,
    causal,
    d_keys,
    d_values,
):
    extent = query.shape[1]

    @pl.when(pl.program_id(0) == 0)
    def _():
        causal[...] = causal_bias(block)

    key_rows, query_rows = extend_rows(lengths[0], extent)
    for head in range(group):
        part = pl.ds(HEAD * head, HEAD)
        keys[head, :HEAD, :] = key[part, :]
        keys[head, HEAD:, :] = key_rows
        queries[head, :HEAD, :] = query[part, :]
        queries[head, HEAD:, :] = query_rows
    for head in range(group):
        part = pl.ds(HEAD * head, HEAD)
        for tile in range(extent // block):
            place = pl.ds(tile * block, block)
            own = queries[head, :, place]
            grade = d_mixture[part, place]
            center = (grade.astype(F32) * mixture[part, place].astype(F32)).sum(0, keepdims=True)
            total = totals[0, pl.ds(head, 1), place]
            d_query = jnp.zeros((HEAD, block), F32)
            for other in range(tile + 1):
                span = pl.ds(other * block, block)
                score = dot(keys[head, :, span], own, 0, 0)
                if other == tile:
                    score = score + causal[...]
                weight = jnp.exp2(score * (SCALE * LOG2E) - total)
                d_weight = dot(value[part, span], grade, 0, 0)
                d_score = (weight * (d_weight - center)).astype(BF)
                d_value = dot(grade, weight.astype(BF), 1, 1)
                d_key = dot(query[part, place], d_score, 1, 1)
                d_query = d_query + dot(key[part, span], d_score, 1, 0)
                if other == tile:
                    d_values[:, span] = d_value
                    d_keys[:, span] = d_key
                else:
                    d_values[:, span] += d_value
                    d_keys[:, span] += d_key
            d_project[0, part, place] = (d_query * SCALE).astype(BF)
        d_project[1, part, :] = (d_keys[...] * SCALE).astype(BF)
        d_project[2, part, :] = d_values[...].astype(BF)


def attention_back_call(lengths, project, mixture, d_mixture, totals):
    extent = project.shape[1]
    group, block = 2, min(512, extent)
    size, steps = HEAD * group, HEADS // group

    def part(section):
        return pl.BlockSpec((size, extent), lambda i: (i + section * steps, 0))

    pairs = extent * extent * 5 // 8
    return pl.pallas_call(
        functools.partial(attention_back_kernel, group, block),
        grid=(steps,),
        in_specs=[SMEM, part(0), part(1), part(2), part(0), part(0)]
        + [pl.BlockSpec((1, group, extent), lambda i: (i, 0, 0))],
        out_specs=pl.BlockSpec((3, size, extent), lambda i: (0, i, 0)),
        out_shape=jax.ShapeDtypeStruct((3, HEADS * HEAD, extent), BF),
        scratch_shapes=[
            pltpu.VMEM((group, HEAD + 16, extent), BF),
            pltpu.VMEM((group, HEAD + 16, extent), BF),
            pltpu.VMEM((block, block), F32),
            pltpu.VMEM((HEAD, extent), F32),
            pltpu.VMEM((HEAD, extent), F32),
        ],
        compiler_params=params(),
        cost_estimate=estimate(30 * HEADS * pairs * HEAD, 16e6, HEADS * pairs),
        name="attention_back",
    )(lengths, project, project, project, mixture, d_mixture, totals)


def first_kernel(counts, tab, d_project, normed, frames, d_middle, gain, *rest):
    count_in, count_grad = counts
    pieces, rest = rest[:count_in], rest[count_in:]
    d_frames, bias_grad, gain_grad, shift_grad = rest[:4]
    grads, rest = rest[4 : 4 + count_grad], rest[4 + count_grad :]
    weight, total, staged, d_normed, sems, sem_total, sems_grad = rest
    step = pl.program_id(0)
    steps = pl.num_programs(0)
    extent, model = normed.shape
    width = d_project.shape[0]

    def fetch(block):
        slot = lax.rem(block, 2)
        return load_columns(pieces, tab, block, weight.at[slot], sems.at[slot], width)

    def send(block):
        slot = lax.rem(block, 2)
        return store_column_block(grads, tab, block, staged.at[slot], sems_grad.at[slot], width)

    def late():
        return pltpu.make_async_copy(d_middle, total, sem_total)

    @pl.when(step == 0)
    def _():
        start(fetch(step))
        late().start()

    @pl.when(step + 1 < steps)
    def _():
        start(fetch(step + 1))

    @pl.when(step >= 2)
    def _():
        wait(send(step - 2))

    now = lax.rem(step, 2)
    staged[now] = dot(normed[...], d_project[...], 0, 1).astype(BF)
    start(send(step))
    bias_grad[...] = dot(jnp.ones((8, extent), BF), d_project[...], 1, 1)[:1, :]
    wait(fetch(step))
    part = dot(d_project[...], weight[now], 0, 1)

    @pl.when(step == 0)
    def _():
        d_normed[...] = part

    @pl.when(step > 0)
    def _():
        d_normed[...] += part

    @pl.when(step == steps - 1)
    def _():
        late().wait()
        gains = jnp.zeros((1, model), F32)
        shifts = jnp.zeros((1, model), F32)
        for first in range(0, extent, ROWS):
            rows = pl.ds(first, ROWS)
            unit, scale = normalise(frames[rows, :].astype(F32))
            grade = d_normed[rows, :]
            gains = gains + (grade * unit).sum(0, keepdims=True)
            shifts = shifts + grade.sum(0, keepdims=True)
            grade = grade * gain[...]
            level = jnp.mean(grade, axis=-1, keepdims=True)
            tilt = jnp.mean(grade * unit, axis=-1, keepdims=True)
            d_frames[rows, :] = (total[rows, :] + scale * (grade - level - unit * tilt)).astype(BF)
        gain_grad[...] = gains
        shift_grad[...] = shifts
        wait(send(step - 1))
        wait(send(step))


def first_call(tab, d_project, normed, frames, d_middle, gain, pieces, spread, sizes):
    extent, model = frames.shape
    width = 3 * model // 4
    grads = gradient_shapes(spread, model, 3 * model, *sizes)
    return pl.pallas_call(
        functools.partial(first_kernel, (len(pieces), len(grads))),
        grid=(4,),
        in_specs=[SMEM, pl.BlockSpec((width, extent), lambda i: (i, 0))]
        + [whole(extent, model), whole(extent, model), ANY, whole(1, model)]
        + [ANY] * len(pieces),
        out_specs=[
            whole(extent, model),
            pl.BlockSpec((1, width), lambda i: (0, i)),
            whole(1, model),
            whole(1, model),
        ]
        + [ANY] * len(grads),
        out_shape=[
            jax.ShapeDtypeStruct((extent, model), BF),
            vec(3 * model),
            vec(model),
            vec(model),
        ]
        + grads,
        scratch_shapes=[
            pltpu.VMEM((2, model, width), BF),
            pltpu.VMEM((extent, model), F32),
            pltpu.VMEM((2, model, width), BF),
            pltpu.VMEM((extent, model), F32),
            pltpu.SemaphoreType.DMA((2, 8)),
            pltpu.SemaphoreType.DMA,
            pltpu.SemaphoreType.DMA((2, 8)),
        ],
        compiler_params=params(),
        cost_estimate=estimate(12 * extent * model * model, 32e6),
        name="first",
    )(tab, d_project, normed, frames, d_middle, gain, *pieces)


def down_kernel(count, tab, active, middle, bias, *rest):
    pieces = rest[:count]
    frames_out, weight, total, sems = rest[count:]
    step = pl.program_id(0)
    steps = pl.num_programs(0)

    def fetch(index):
        slot = index % 2
        return load_rows(pieces, tab, index, weight.at[slot], sems.at[slot])

    def body(index):
        if index == 0:
            start(fetch(0))
        if index + 1 < 4:
            start(fetch(index + 1))
        wait(fetch(index))
        part = dot(active[...], weight[index % 2], 1, 0)
        if index == 0:
            total[...] = part
        elif index < 3:
            total[...] += part
        else:
            frames_out[...] = (total[...] + part + (middle[...] + bias[...])).astype(BF)

    for index in range(4):
        pl.when(step == index)(functools.partial(body, index))


def down_call(tab, active, middle, bias, pieces):
    extent, hidden = active.shape
    model = middle.shape[1]
    grid = pltpu.PrefetchScalarGridSpec(
        num_scalar_prefetch=1,
        grid=(hidden // TILE,),
        in_specs=[pl.BlockSpec((extent, TILE), lambda i, tab: (0, tab[T_PAIR + i]))]
        + [whole(extent, model), whole(1, model)]
        + [ANY] * len(pieces),
        out_specs=whole(extent, model),
        scratch_shapes=[
            pltpu.VMEM((2, TILE, model), BF),
            pltpu.VMEM((extent, model), F32),
            pltpu.SemaphoreType.DMA((2, 8)),
        ],
    )
    return pl.pallas_call(
        functools.partial(down_kernel, len(pieces)),
        grid_spec=grid,
        out_shape=jax.ShapeDtypeStruct((extent, model), BF),
        compiler_params=params(),
        cost_estimate=estimate(8 * extent * model * model, 24e6),
        name="down",
    )(tab, active, middle, bias, *pieces)


def gather_plain(weight):
    wide = lax.all_gather(weight, "inner", axis=1, tiled=True)
    return [lax.all_gather(wide, "dp", axis=0, tiled=True)]


def scatter_plain(grads):
    wide = lax.psum_scatter(grads[0], "dp", scatter_dimension=0, tiled=True)
    return lax.psum_scatter(wide, "inner", scatter_dimension=1, tiled=True).astype(F32)


def shards(
    spread,
    sizes,
    frames_in,
    lengths,
    first_gain,
    first_shift,
    attend_weight,
    attend_bias,
    output_weight,
    output_bias,
    second_gain,
    second_shift,
    up_weight,
    up_bias,
    down_weight,
    down_bias,
    cotangent,
):
    _, extent, model = frames_in.shape
    frames = frames_in.reshape(extent, model)
    upstream = cotangent.reshape(extent, model)
    tab = make_table(spread)

    def row(vector):
        return vector.reshape(1, -1)

    attend_pieces = gather_plain(attend_weight)
    out_pieces = gather_plain(output_weight)
    up_pieces = gather_plain(up_weight)
    down_pieces = gather_plain(down_weight)
    bias_row = jnp.concatenate([attend_bias[0], jnp.zeros_like(attend_bias[0]), attend_bias[1]])
    normed, project = project_call(
        tab, frames, row(first_gain), row(first_shift), row(bias_row), attend_pieces
    )
    mixture, totals = attention_call(lengths, project)
    vectors = (row(output_bias), row(second_gain), row(second_shift), row(up_bias))
    middle, normed_two, active, slope, grad_down_bias, *down_grads = up_call(
        tab,
        lengths,
        mixture,
        frames,
        upstream,
        vectors,
        out_pieces,
        up_pieces,
        spread,
        sizes,
    )
    (
        d_middle,
        d_mixture,
        grad_up_bias,
        grad_second_gain,
        grad_second_shift,
        grad_output_bias,
        *back_grads,
    ) = back_call(
        tab,
        lengths,
        mixture,
        middle,
        normed_two,
        upstream,
        slope,
        row(second_gain),
        (out_pieces, up_pieces, down_pieces),
        spread,
        sizes,
    )
    d_project = attention_back_call(lengths, project, mixture, d_mixture, totals)
    d_frames, grad_bias, grad_first_gain, grad_first_shift, *attend_grads = first_call(
        tab,
        d_project.reshape(3 * model, extent),
        normed,
        frames,
        d_middle,
        row(first_gain),
        attend_pieces,
        spread,
        sizes,
    )
    frames_out = down_call(tab, active, middle, row(down_bias), down_pieces)
    down_owned = scatter_plain(down_grads)
    up_owned = scatter_plain(back_grads[:1])
    output_owned = scatter_plain(back_grads[1:])
    attend_owned = scatter_plain(attend_grads)
    small = lax.psum(
        jnp.concatenate(
            [
                grad_first_gain,
                grad_first_shift,
                grad_bias[:, :model],
                grad_bias[:, 2 * model :],
                grad_output_bias,
                grad_second_gain,
                grad_second_shift,
                grad_down_bias,
                grad_up_bias,
            ],
            axis=1,
        ),
        ("dp", "inner"),
    ).reshape(-1)

    def take(first, count=1):
        return small[first * model : (first + count) * model]

    return (
        frames_out.reshape(frames_in.shape),
        d_frames.reshape(frames_in.shape),
        take(0),
        take(1),
        attend_owned,
        take(2, 2).reshape(2, model),
        output_owned,
        take(4),
        take(5),
        take(6),
        up_owned,
        take(8, 4),
        down_owned,
        take(7),
    )


def solution(mesh):
    sizes = (mesh.shape["dp"], mesh.shape["inner"])
    spread = False
    return jax.shard_map(
        functools.partial(shards, spread, sizes),
        mesh=mesh,
        in_specs=(
            P(("dp", "inner"), None, None),
            P(("dp", "inner")),
            P(),
            P(),
            P("dp", "inner"),
            P(),
            P("dp", "inner"),
            P(),
            P(),
            P(),
            P("dp", "inner"),
            P(),
            P("dp", "inner"),
            P(),
            P(("dp", "inner"), None, None),
        ),
        out_specs=(
            P(("dp", "inner"), None, None),
            P(("dp", "inner"), None, None),
            P(),
            P(),
            P("dp", "inner"),
            P(),
            P("dp", "inner"),
            P(),
            P(),
            P(),
            P("dp", "inner"),
            P(),
            P("dp", "inner"),
            P(),
        ),
        check_vma=False,
    )
```

time: 993 us -> 730 us (0.74)
  matrix products: 322 us -> 0 us
  Pallas kernels: 0 us -> 225 us
  other arithmetic: 89.4 us -> 7.37 us
  local copies, waits for them, and re-layouts: 58.9 us -> 1.99 us
  waiting for transfers between devices: 415 us -> 389 us
    dot_general x24 -> x0, matrix products: 322 us -> none  [the longest x4 56 us: contract_cols(): lax.dot_general(left, right, (((1,), (1,)), ((), ())), preferred_element_...]
    pallas_call x0 -> x7, Pallas kernels: none -> 225 us  [the longest x1 72.1 us: back_call(): pl.pallas_call(functools.partial(back_kernel, (len(out_pieces), len(up_pi...]
    reduce_scatter x8, waiting for transfers between devices: 352 us -> 249 us  [the longest x4 209 us: scatter_plain(): wide = lax.psum_scatter(grads[0], 'dp', scatter_dimension=0, tiled=True)]
    all_gather x6, waiting for transfers between devices: 60.7 us -> 137 us  [the longest x4 110 us: gather_plain(): return [lax.all_gather(wide, 'dp', axis=0, tiled=True)]]
    reduce_sum x12 -> x0, other arithmetic: 46.4 us -> none  [the longest x2 23.7 us: attention_forward(): summed = jnp.sum(weights, axis=-1, keepdims=True)]
    convert_element_type x3 -> x4, other arithmetic: 38.4 us -> 6.77 us  [scatter_plain(): lax.psum_scatter(wide, 'inner', scatter_dimension=1, tiled=True).astype(F32)]
    unnamed x146 -> x26, local copies, waits for them, and re-layouts: 26.9 us -> 0.12 us
    slice x11 -> x4, local copies, waits for them, and re-layouts: 21.2 us -> 1.25 us  [the longest x3 1.25 us: take(): return small[first * model:(first + count) * model]]
  transfers between devices with their start and end apart: 14 -> 14, of which waited for: 7 -> 9; matrix products, arithmetic and copies ran while one was open for 40% -> 1% of each run, Pallas kernels for 0% -> 21%
where the time goes in v1:
time: 730 us; the launch traced here: 724 us
  waiting for transfers between devices  389 us (53%)
  Pallas kernels  225 us (31%)
  blocking collectives  85.1 us (12%)
  between operations  15.1 us (2%)
  other arithmetic  7.37 us (1%)
    reduce_scatter x4, waiting for transfers between devices, scatter_plain(): wide = lax.psum_scatter(grads[0], 'dp', scatter_dimension=0, tiled=True)  209 us
    all_gather x4, waiting for transfers between devices, gather_plain(): return [lax.all_gather(wide, 'dp', axis=0, tiled=True)]  110 us
    pallas_call x1, Pallas kernels, back_call(): pl.pallas_call(functools.partial(back_kernel, (len(out_pieces), len(up_pi...  72.1 us
    all_gather x2, blocking collectives, gather_plain(): wide = lax.all_gather(weight, 'inner', axis=1, tiled=True)  45.1 us
    psum x1, blocking collectives, shards(): lax.psum(jnp.concatenate([grad_first_gain, grad_first_shift, grad_bias[:,...  40 us
    reduce_scatter x4, waiting for transfers between devices, scatter_plain(): lax.psum_scatter(wide, 'inner', scatter_dimension=1, tiled=True).astype(F32)  39.5 us
    pallas_call x1, Pallas kernels, up_call(): pl.pallas_call(functools.partial(up_kernel, (len(out_pieces), len(up_piec...  38.4 us
    pallas_call x1, Pallas kernels, attention_back_call(): pl.pallas_call(functools.partial(attention_back_kernel, group, block), gr...  34.5 us
  transfers between devices with their start and end apart: 14, of which 9 were waited for; matrix products, arithmetic and copies ran while one was open for 1% of the time, Pallas kernels for 21%

profile of v1, /device:TPU:0, one launch (start us, length us, event | category | flops | bytes accessed | tf_op | source)
XLA Modules:
  0.0 724.1 jit_solution(3424127368477813501)
XLA Ops:
  7.2 0.0 all-gather.11.cloned.1.call-start
  7.2 0.7 all-gather.11.cloned.1.call-update
  7.9 0.0 all-gather.15.cloned.1.call-start
  8.0 0.7 all-gather.15.cloned.1.call-update
  8.7 0.0 all-gather.7.cloned.1.call-start
  8.7 27.2 %all_gather.24 = bf16[128,3072]{1,0:T(8,128)(2,1)} all-gather(bf16[128,768]{1,0:T(8,128)(2,1)} %param.20), channel_id=1, replica_groups=mesh['dp'=8,'inner'=4] {'inner'}, dimensions={1}, use_global_device_ids=true | all-gather | bytes 983040 | tf_op jit(solution)/shard_map/all_gather | solution.py:974
  35.9 0.0 all-gather.9.cloned.1.call-start
  36.0 17.9 %all_gather.26 = bf16[128,1024]{1,0:T(8,128)(2,1)} all-gather(bf16[128,256]{1,0:T(8,128)(2,1)} %param.22), channel_id=1, replica_groups=mesh['dp'=8,'inner'=4] {'inner'}, dimensions={1}, use_global_device_ids=true | all-gather | bytes 327680 | tf_op jit(solution)/shard_map/all_gather | solution.py:974
  53.9 0.0 all-gather.13.cloned.1.call-start
  54.0 0.5 all-gather.13.cloned.1.call-update
  54.5 0.0 all-gather.17.cloned.1.call-start
  54.6 26.4 %all-gather.15.cloned.1.call-done = bf16[512,1024]{1,0:T(8,128)(2,1)} async-done(((bf16[512,256]{1,0:T(8,128)(2,1)}), bf16[512,1024]{1,0:T(8,128)(2,1)}) %all-gather.15.cloned.1.call-update) | async-done | bytes 1048592 | tf_op jit(solution)/shard_map/all_gather | solution.py:974
  81.0 0.0 reduce-scatter.13.cloned.1.call-start
  81.7 0.6 pad_maximum_fusion
  82.3 44.4 %all-gather.7.cloned.1.call-done.rest_0_ = bf16[1024,3072]{1,0:T(8,128)(2,1)} async-done(((bf16[128,3072]{1,0:T(8,128)(2,1)}), bf16[1024,3072]{1,0:T(8,128)(2,1)}) %all-gather.7.cloned.1.call-update) | async-done | bytes 6291472 | tf_op jit(solution)/shard_map/all_gather | solution.py:975
  126.7 12.7 %project.1 = (bf16[1024,1024]{1,0:T(8,128)(2,1)}, bf16[3072,1024]{1,0:T(8,128)(2,1)}) custom-call(s32[48]{0:T(128)} %constant.4.clone.tab, bf16[1024,1024]{1,0:T(8,128)(2,1)} %bitcast.34, f32[1,1024]{1,0:T(1,128)} %bitcast.43, f32[1,1024]{1,0:T(1,128)} %bitcast.38, f32[1,3072]{1,0:T(1,128)} %bitcast.25, bf16[1024,3072]{1,0:T(8,128)(2,1)} %all-gather.7.cloned.1.call-done.rest_0_), custom_call_target="tpu_custom_call" | custom-call | flops 6442450944 | bytes 16000000 | tf_op jit(solution)/shard_map/project/pallas_call | solution.py:258
  139.4 25.0 %attention.1 = (bf16[1024,1024]{1,0:T(8,128)(2,1)}, f32[8,2,1024]{2,1,0:T(2,128)}) custom-call(s32[1]{0:T(128)S(6)} %copy.38.lengths, bf16[3072,1024]{1,0:T(8,128)(2,1)} %get-tuple-element.37.query.key.value, bf16[3072,1024]{1,0:T(8,128)(2,1)} %get-tuple-element.37.query.key.value, bf16[3072,1024]{1,0:T(8,128)(2,1)} %get-tuple-element.37.query.key.value), custom_call_target="tpu_custom_call" | custom-call | flops 10737418240 | bytes 8000000 | tf_op jit(solution)/shard_map/attention/pallas_call | solution.py:343
  164.4 48.2 %all-gather.13.cloned.1.call-done.rest_5_.rest_2_ = bf16[1024,4096]{1,0:T(8,128)(2,1)} async-done(((bf16[128,4096]{1,0:T(8,128)(2,1)}), bf16[1024,4096]{1,0:T(8,128)(2,1)}) %all-gather.13.cloned.1.call-update) | async-done | bytes 8388624 | tf_op jit(solution)/shard_map/all_gather | solution.py:975
  212.6 38.4 %up.1 = (f32[1024,1024]{1,0:T(8,128)}, bf16[1024,1024]{1,0:T(8,128)(2,1)}, bf16[1024,4096]{1,0:T(8,128)(2,1)}, bf16[1024,4096]{1,0:T(8,128)(2,1)}, f32[1,1024]{1,0:T(1,128)}, /*index=5*/bf16[4096,1024]{1,0:T(8,128)(2,1)}) custom-call(s32[48]{0:T(128)} %constant.4.clone.tab, s32[1]{0:T(128)S(6)} %copy.38.lengths, ...), custom_call_target="tpu_custom_call" | custom-call | flops 19327352832 | bytes 50000000 | tf_op jit(solution)/shard_map/up/pallas_call | solution.py:457
  251.0 17.8 %all-gather.17.cloned.1.call-done.rest_0_.rest_3_ = bf16[4096,1024]{1,0:T(8,128)(2,1)} async-done(((bf16[512,1024]{1,0:T(8,128)(2,1)}), bf16[4096,1024]{1,0:T(8,128)(2,1)}) %all-gather.17.cloned.1.call-update) | async-done | bytes 8388624 | tf_op jit(solution)/shard_map/all_gather | solution.py:975
  268.8 72.1 %back.1 = (f32[1024,1024]{1,0:T(8,128)}, bf16[1024,1024]{1,0:T(8,128)(2,1)}, f32[1,4096]{1,0:T(1,128)}, f32[1,1024]{1,0:T(1,128)}, f32[1,1024]{1,0:T(1,128)}, /*...) custom-call(s32[48]{0:T(128)} %constant.4.clone.tab, s32[1]{0:T(128)S(6)} %copy.38.lengths, ...), custom_call_target="tpu_custom_call" | custom-call | flops 30064771072 | bytes 60000000 | tf_op jit(solution)/shard_map/back/pallas_call | solution.py:687
  340.9 0.0 reduce-scatter.9.cloned.1.call-start
  340.9 34.5 %attention_back.1 = bf16[3,1024,1024]{2,1,0:T(8,128)(2,1)} custom-call(s32[1]{0:T(128)S(6)} %copy.38.lengths, bf16[3072,1024]{1,0:T(8,128)(2,1)} %get-tuple-element.37.query.key.value, bf16[3072,1024]{1,0:T(8,128)(2,1)} %get-tuple-element.37.query.key.value, bf16[3072,1024]{1,0:T(8,128)(2,1)} %get-tuple-element.37.query.key.value, ...), custom_call_target="tpu_custom_call" | custom-call | flops 20132659200 | bytes 16000000 | tf_op jit(solution)/shard_map/attention_back/pallas_call | solution.py:789
  375.5 25.6 %first.1 = (bf16[1024,1024]{1,0:T(8,128)(2,1)}, f32[1,3072]{1,0:T(1,128)}, f32[1,1024]{1,0:T(1,128)}, f32[1,1024]{1,0:T(1,128)}, bf16[1024,3072]{1,0:T(8,128)(2,1)}) custom-call(s32[48]{0:T(128)} %constant.4.clone.tab, bf16[3072,1024]{1,0:T(8,128)(2,1)} %bitcast.46, bf16[1024,1024]{1,0:T(8,128)(2,1)} %get-tuple-element.45.normed, ...), custom_call_target="tpu_custom_call" | custom-call | flops 12884901888 | bytes 32000000 | tf_op jit(solution)/shard_map/first/pallas_call | solution.py:884
  401.1 0.0 reduce-scatter.21.cloned.1.call-start
  401.2 0.7 reduce-scatter.21.cloned.1.call-update
  401.9 0.0 reduce-scatter.17.cloned.1.call-start
  402.0 0.4 reduce-scatter.17.cloned.1.call-update
  402.5 0.0 reduce-scatter.15.cloned.1.call-start
  402.5 0.7 reduce-scatter.15.cloned.1.call-update
  403.2 0.0 reduce-scatter.11.cloned.1.call-start
  403.2 59.8 %reduce-scatter.9.cloned.1.call-done = bf16[128,3072]{1,0:T(8,128)(2,1)} async-done(((bf16[1024,3072]{1,0:T(8,128)(2,1)}), bf16[128,3072]{1,0:T(8,128)(2,1)}) %reduce-scatter.9.cloned.1.call-update) | async-done | bytes 786448 | tf_op jit(solution)/shard_map/reduce_scatter | solution.py:979
  463.1 0.0 reduce-scatter.23.cloned.1.call-start
  463.2 74.7 %reduce-scatter.21.cloned.1.call-done = bf16[512,1024]{1,0:T(8,128)(2,1)} async-done(((bf16[4096,1024]{1,0:T(8,128)(2,1)}), bf16[512,1024]{1,0:T(8,128)(2,1)}) %reduce-scatter.21.cloned.1.call-update) | async-done | bytes 1048592 | tf_op jit(solution)/shard_map/reduce_scatter | solution.py:979
  537.9 0.0 reduce-scatter.19.cloned.1.call-start
  538.0 74.9 %reduce-scatter.17.cloned.1.call-done = bf16[128,4096]{1,0:T(8,128)(2,1)} async-done(((bf16[1024,4096]{1,0:T(8,128)(2,1)}), bf16[128,4096]{1,0:T(8,128)(2,1)}) %reduce-scatter.17.cloned.1.call-update) | async-done | bytes 1048592 | tf_op jit(solution)/shard_map/reduce_scatter | solution.py:979
  613.0 40.0 %psum.7 = f32[1,12288]{1,0:T(1,128)S(1)} all-reduce(f32[1,12288]{1,0:T(1,128)S(1)} %constant_dynamic-update-slice_fusion), channel_id=1, replica_groups=mesh['dp'=8,'inner'=4] {'dp','inner'}, use_global_device_ids=true, to_apply=%region_0.0 | all-reduce | flops 12288 | bytes 98304 | tf_op jit(solution)/shard_map/psum | solution.py:1070
  653.0 0.6 slice.83
  653.7 0.6 reshape.95
  654.3 0.6 fusion
  654.9 16.2 %down.1 = bf16[1024,1024]{1,0:T(8,128)(2,1)} custom-call(s32[48]{0:T(128)} %constant.4.clone.tab, bf16[1024,4096]{1,0:T(8,128)(2,1)} %get-tuple-element.39.active, f32[1024,1024]{1,0:T(8,128)} %get-tuple-element.40.middle, f32[1,1024]{1,0:T(1,128)} %bitcast.45, bf16[4096,1024]{1,0:T(8,128)(2,1)} %all-gather.17.cloned.1.call-done.rest_0_.rest_3_), custom_call_target="tpu_custom_call" | custom-call | flops 8589934592 | bytes 24000000 | tf_op jit(solution)/shard_map/down/pallas_call | solution.py:963
  671.1 0.0 reduce-scatter.15.cloned.1.call-done
  671.2 1.5 convert_element_type.13
  672.7 1.7 convert_element_type.12
  674.4 13.3 %reduce-scatter.23.cloned.1.call-done = bf16[512,256]{1,0:T(8,128)(2,1)} async-done(((bf16[512,1024]{1,0:T(8,128)(2,1)}), bf16[512,256]{1,0:T(8,128)(2,1)}) %reduce-scatter.23.cloned.1.call-update) | async-done | bytes 262160 | tf_op jit(solution)/shard_map/reduce_scatter | solution.py:980
  687.6 1.8 convert_element_type.15
  689.4 26.2 %reduce-scatter.19.cloned.1.call-done = bf16[128,1024]{1,0:T(8,128)(2,1)} async-done(((bf16[128,4096]{1,0:T(8,128)(2,1)}), bf16[128,1024]{1,0:T(8,128)(2,1)}) %reduce-scatter.19.cloned.1.call-update) | async-done | bytes 262160 | tf_op jit(solution)/shard_map/reduce_scatter | solution.py:980
  715.6 1.8 convert_element_type.14
  (42 shorter events, 0.3 us)
Async XLA Ops:
  7.2 74.5 %copy-start.1 = (f32[2,1024]{1,0:T(2,128)S(1)}, f32[2,1024]{1,0:T(2,128)}, u32[]{:S(2)}) copy-start(f32[2,1024]{1,0:T(2,128)} %param.21) | copy-start | bytes 24580
  7.2 46.8 %all-gather.11.cloned.1.call-start = ((), (), s32[]{:S(2)}) async-start(), calls=%async_computation.10 | async-start | bytes 1310720 | tf_op jit(solution)/shard_map/all_gather | solution.py:974
  7.9 73.0 %all-gather.15.cloned.1.call-start = ((), (), s32[]{:S(2)}) async-start(), calls=%async_computation.12 | async-start | bytes 1310720 | tf_op jit(solution)/shard_map/all_gather | solution.py:974
  8.7 118.1 %all-gather.7.cloned.1.call-start = ((), (), s32[]{:S(2)}) async-start(), calls=%async_computation.8 | async-start | bytes 7077888 | tf_op jit(solution)/shard_map/all_gather | solution.py:975
  35.9 128.5 %all-gather.9.cloned.1.call-start = ((), (), s32[]{:S(2)}) async-start(), calls=%async_computation.9 | async-start | bytes 2359296 | tf_op jit(solution)/shard_map/all_gather | solution.py:975
  53.9 158.7 %all-gather.13.cloned.1.call-start = ((), (), s32[]{:S(2)}) async-start(), calls=%async_computation.11 | async-start | bytes 9437184 | tf_op jit(solution)/shard_map/all_gather | solution.py:975
  54.5 214.2 %all-gather.17.cloned.1.call-start = ((), (), s32[]{:S(2)}) async-start(), calls=%async_computation.13 | async-start | bytes 9437184 | tf_op jit(solution)/shard_map/all_gather | solution.py:975
  81.0 321.5 %reduce-scatter.13.cloned.1.call-start = ((), (), s32[]{:S(2)}) async-start(), calls=%async_computation.16 | async-start | bytes 2359296 | tf_op jit(solution)/shard_map/reduce_scatter | solution.py:979
  340.9 122.2 %reduce-scatter.9.cloned.1.call-start = ((), (), s32[]{:S(2)}) async-start(), calls=%async_computation.14 | async-start | bytes 7077888 | tf_op jit(solution)/shard_map/reduce_scatter | solution.py:979
  401.1 136.7 %reduce-scatter.21.cloned.1.call-start = ((), (), s32[]{:S(2)}) async-start(), calls=%async_computation.20 | async-start | bytes 9437184 | tf_op jit(solution)/shard_map/reduce_scatter | solution.py:979
  401.9 211.0 %reduce-scatter.17.cloned.1.call-start = ((), (), s32[]{:S(2)}) async-start(), calls=%async_computation.18 | async-start | bytes 9437184 | tf_op jit(solution)/shard_map/reduce_scatter | solution.py:979
  401.9 136.0 %copy-start.8 = (f32[1,1024]{1,0:T(1,128)S(1)}, f32[1,1024]{1,0:T(1,128)}, u32[]{:S(2)}) copy-start(f32[1,1024]{1,0:T(1,128)} %get-tuple-element.48) | copy-start | bytes 12292
  401.9 136.0 %copy-start.7 = (f32[1,1024]{1,0:T(1,128)S(1)}, f32[1,1024]{1,0:T(1,128)}, u32[]{:S(2)}) copy-start(f32[1,1024]{1,0:T(1,128)} %get-tuple-element.49) | copy-start | bytes 12292
  401.9 136.0 %copy-start.2 = (f32[1,3072]{1,0:T(1,128)S(1)}, f32[1,3072]{1,0:T(1,128)}, u32[]{:S(2)}) copy-start(f32[1,3072]{1,0:T(1,128)} %get-tuple-element.50) | copy-start | bytes 36868
  402.0 210.9 %copy-start.6 = (f32[1,1024]{1,0:T(1,128)S(1)}, f32[1,1024]{1,0:T(1,128)}, u32[]{:S(2)}) copy-start(f32[1,1024]{1,0:T(1,128)} %get-tuple-element.51) | copy-start | bytes 12292
  402.0 210.9 %copy-start.5 = (f32[1,1024]{1,0:T(1,128)S(1)}, f32[1,1024]{1,0:T(1,128)}, u32[]{:S(2)}) copy-start(f32[1,1024]{1,0:T(1,128)} %get-tuple-element.52) | copy-start | bytes 12292
  402.0 211.0 %copy-start.4 = (f32[1,1024]{1,0:T(1,128)S(1)}, f32[1,1024]{1,0:T(1,128)}, u32[]{:S(2)}) copy-start(f32[1,1024]{1,0:T(1,128)} %get-tuple-element.53) | copy-start | bytes 12292
  402.0 211.0 %copy-start.3 = (f32[1,1024]{1,0:T(1,128)S(1)}, f32[1,1024]{1,0:T(1,128)}, u32[]{:S(2)}) copy-start(f32[1,1024]{1,0:T(1,128)} %get-tuple-element.54) | copy-start | bytes 12292
  402.0 211.0 %copy-start = (f32[1,4096]{1,0:T(1,128)S(1)}, f32[1,4096]{1,0:T(1,128)}, u32[]{:S(2)}) copy-start(f32[1,4096]{1,0:T(1,128)} %get-tuple-element.55) | copy-start | bytes 49156
  402.5 268.7 %reduce-scatter.15.cloned.1.call-start = ((), (), s32[]{:S(2)}) async-start(), calls=%async_computation.17 | async-start | bytes 327680 | tf_op jit(solution)/shard_map/reduce_scatter | solution.py:980
  403.2 269.5 %reduce-scatter.11.cloned.1.call-start = ((), (), s32[]{:S(2)}) async-start(), calls=%async_computation.15 | async-start | bytes 983040 | tf_op jit(solution)/shard_map/reduce_scatter | solution.py:980
  463.1 224.5 %reduce-scatter.23.cloned.1.call-start = ((), (), s32[]{:S(2)}) async-start(), calls=%async_computation.21 | async-start | bytes 1310720 | tf_op jit(solution)/shard_map/reduce_scatter | solution.py:980
  537.9 177.7 %reduce-scatter.19.cloned.1.call-start = ((), (), s32[]{:S(2)}) async-start(), calls=%async_computation.19 | async-start | bytes 1310720 | tf_op jit(solution)/shard_map/reduce_scatter | solution.py:980
Sparse Core Ops, SparseCore 0:
  9.6 39.6 all-gather.10
  50.9 30.0 all-gather.14
  82.9 43.8 all-gather.6
  128.5 27.9 all-gather.8
  158.2 54.3 all-gather.12
  214.3 54.3 all-gather.16
  341.0 41.3 reduce-scatter.12
  401.3 61.7 reduce-scatter.8
  466.5 71.2 reduce-scatter.20
  541.6 71.2 reduce-scatter.16
  615.1 19.6 reduce-scatter.14
  637.1 21.6 reduce-scatter.10
  661.2 26.3 reduce-scatter.22
  689.8 25.7 reduce-scatter.18
